TPU v7x, 32 devices: a whole 2x2x4 slice. The times are simulated.
32 devices in a mesh: panel: 2 (over x), lon: 8 (over z, y), colat: 2 (over core).
Axes of the slice: x: 2, y: 2, z: 4, core: 2. Of those that a mesh axis runs over, the one named last changes fastest.
Arguments:
- flow_vector: float32 [2, 3, 16, 192, 128], P('panel', None, 'colat', 'lon'), may hold values from -6 to 6
- mean_stress: float32 [2, 16, 192, 128], P('panel', 'colat', 'lon'), may hold values from -6 to 6
- shear_resistance: float32 [2, 16, 192, 128], P('panel', 'colat', 'lon'), may hold values from 0.3 to 30
- thermal_anomaly: float32 [2, 16, 192, 128], P('panel', 'colat', 'lon'), may hold values from -6 to 6
- source_azimuth_portion: int32 [2, 416], P('panel'), may hold values from 0 to 7, as said below
- source_first_slot: int32 [2, 416], P('panel'), may hold values from 0 to 166, as said below
- source_bilinear_weights: float32 [2, 2, 416], P('panel'), may hold values from 0 to 1
- source_frame_rotation: float32 [2, 416], P('panel'), may hold values from -3.140625 to 3.140625
Outputs:
- velocity_out: float32 [2, 3, 16, 192, 128], P('panel', None, 'colat', 'lon')
- pressure_out: float32 [2, 16, 192, 128], P('panel', 'colat', 'lon')
Inputs may be any that keep to these rules, and one draw needn't show every extreme that they name: `source_azimuth_portion`: the donors of border row r lie in the colatitude shard of that border row. Within one colatitude shard of a panel, no longitude shard is named by more than 26 border rows, and in the first and last colatitude shard one is named exactly 26 times. Among the border rows whose ghost cells lie in one longitude shard, no longitude shard is named more than 4 times, and in the first and last colatitude shard some is named exactly 4 times. `source_first_slot`: the value v names the cell (v // 24, v mod 24) of the donor shard, with v // 24 <= 6 and v mod 24 <= 22, so that all four donor cells lie in that shard.
All inputs are finite; a program needn't handle non-finite values.
Results may differ from a plain program's by a relative error of at most 0.00002.
Values sent between devices are 32-bit elements; how exact they have to be, the bound alone decides.
A program may use at most 64 MiB of HBM per device.

v0:
```python
import math

import jax
import jax.numpy as jnp
from jax import lax
from jax.sharding import PartitionSpec as P

SWEEPS = 2


OMEGA_VELOCITY = 0.8
OMEGA_PRESSURE = 0.1
INNER_RATIO = 11.0 / 9.0


def partner(block, axis, apart):
    count = lax.axis_size(axis)
    route = []
    for low in range(count):
        high = low | 1 << apart
        if high != low and high < count:
            route += [(low, high), (high, low)]
    return lax.ppermute(block, axis, route)


def extended(cells, sides, width):
    for axis, dim in sides:
        count = lax.axis_size(axis)
        ends = count - 1
        head = lax.slice_in_dim(cells, 0, width, axis=dim)
        tail = lax.slice_in_dim(cells, cells.shape[dim] - width, cells.shape[dim], axis=dim)
        cells = jnp.concatenate(
            [
                lax.ppermute(tail, axis, [(i, (i + 1) % count) for i in range(ends)]),
                cells,
                lax.ppermute(head, axis, [((i + 1) % count, i) for i in range(ends)]),
            ],
            axis=dim,
        )
    return cells


def shift_up(values):
    return jnp.concatenate([values[..., 1:], jnp.zeros_like(values[..., :1])], axis=-1)


def shift_down(values):
    return jnp.concatenate([jnp.zeros_like(values[..., :1]), values[..., :-1]], axis=-1)


def blend_rotate(
    corner_first, corner_east, corner_south, corner_last, along_polar, along_azimuth, turn_angle
):
    weight_polar = along_polar[None, :, None]
    weight_azimuth = along_azimuth[None, :, None]
    blended = (
        (1.0 - weight_polar) * (1.0 - weight_azimuth) * corner_first
        + (1.0 - weight_polar) * weight_azimuth * corner_east
        + weight_polar * (1.0 - weight_azimuth) * corner_south
        + weight_polar * weight_azimuth * corner_last
    )
    cosine_turn = jnp.cos(turn_angle)[:, None]
    sine_turn = jnp.sin(turn_angle)[:, None]
    polar_part = cosine_turn * blended[1] + sine_turn * blended[2]
    azimuth_part = cosine_turn * blended[2] - sine_turn * blended[1]
    return jnp.concatenate([blended[:1], polar_part[None], azimuth_part[None], blended[3:]], axis=0)


def weighted_smoothing_pass(
    vel_pad,
    pres_pad,
    viscosity_padded,
    buoyant_temp,
    colatitude_value,
    inner_shell_radius,
    colatitude_spacing,
    longitude_spacing,
):
    radial_count = vel_pad.shape[-1]
    radius = inner_shell_radius + jnp.arange(radial_count, dtype=jnp.float32) + 0.5
    sine_values = jnp.sin(colatitude_value)
    sine_centre = sine_values[1:-1][:, None, None]
    sine_north = jnp.sin(colatitude_value[1:-1] - 0.5 * colatitude_spacing)[:, None, None]
    sine_south = jnp.sin(colatitude_value[1:-1] + 0.5 * colatitude_spacing)[:, None, None]
    visc_centre = viscosity_padded[1:-1, 1:-1]
    visc_above = jnp.concatenate([visc_centre[..., 1:], visc_centre[..., -1:]], axis=-1)
    visc_below = jnp.concatenate([visc_centre[..., :1], visc_centre[..., :-1]], axis=-1)
    polar_step = radius * colatitude_spacing
    azimuth_step = radius * sine_centre * longitude_spacing
    coef_above = 0.5 * (visc_centre + visc_above) * ((radius + 0.5) / radius) ** 2
    coef_below = 0.5 * (visc_centre + visc_below) * ((radius - 0.5) / radius) ** 2
    coef_north = (
        0.5
        * (visc_centre + viscosity_padded[:-2, 1:-1])
        * (sine_north / sine_centre)
        / polar_step**2
    )
    coef_south = (
        0.5
        * (visc_centre + viscosity_padded[2:, 1:-1])
        * (sine_south / sine_centre)
        / polar_step**2
    )
    coef_west = 0.5 * (visc_centre + viscosity_padded[1:-1, :-2]) / azimuth_step**2
    coef_east = 0.5 * (visc_centre + viscosity_padded[1:-1, 2:]) / azimuth_step**2
    diagonal = coef_above + coef_below + coef_north + coef_south + coef_west + coef_east
    pres_centre = pres_pad[1:-1, 1:-1]
    grad_radial = 0.5 * (shift_up(pres_centre) - shift_down(pres_centre))
    grad_polar = 0.5 * (pres_pad[2:, 1:-1] - pres_pad[:-2, 1:-1]) / polar_step
    grad_azimuth = 0.5 * (pres_pad[1:-1, 2:] - pres_pad[1:-1, :-2]) / azimuth_step
    forcing = (buoyant_temp - grad_radial, -grad_polar, -grad_azimuth)
    updated = []
    for component in range(3):
        field_pad = vel_pad[component]
        centre = field_pad[1:-1, 1:-1]
        viscous = (
            coef_above * (shift_up(centre) - centre)
            + coef_below * (shift_down(centre) - centre)
            + coef_north * (field_pad[:-2, 1:-1] - centre)
            + coef_south * (field_pad[2:, 1:-1] - centre)
            + coef_west * (field_pad[1:-1, :-2] - centre)
            + coef_east * (field_pad[1:-1, 2:] - centre)
        )
        updated.append(centre + OMEGA_VELOCITY * (forcing[component] + viscous) / diagonal)
    radial_vel = vel_pad[0, 1:-1, 1:-1]
    div_radial = (
        0.5
        * (
            (radius + 1.0) ** 2 * shift_up(radial_vel)
            - (radius - 1.0) ** 2 * shift_down(radial_vel)
        )
        / radius**2
    )
    div_polar = (
        0.5
        * (
            sine_values[2:, None, None] * vel_pad[1, 2:, 1:-1]
            - sine_values[:-2, None, None] * vel_pad[1, :-2, 1:-1]
        )
        / (polar_step * sine_centre)
    )
    div_azimuth = 0.5 * (vel_pad[2, 1:-1, 2:] - vel_pad[2, 1:-1, :-2]) / azimuth_step
    divergence = div_radial + div_polar + div_azimuth
    smoothed_mean_stress = pres_centre - OMEGA_PRESSURE * visc_centre * divergence
    return (jnp.stack(updated, axis=0), smoothed_mean_stress)


def body(
    flow_vector,
    mean_stress,
    shear_resistance,
    thermal_anomaly,
    source_azimuth_portion,
    source_first_slot,
    source_bilinear_weights,
    source_frame_rotation,
):
    polar_cells = flow_vector.shape[2]
    azimuth_cells = flow_vector.shape[3]
    radial_cells = flow_vector.shape[4]
    lon_count = lax.axis_size("lon")
    colat_count = lax.axis_size("colat")
    lon_place = lax.axis_index("lon")
    colat_place = lax.axis_index("colat")
    polar_total = polar_cells * colat_count
    azimuth_total = azimuth_cells * lon_count
    border_rows = source_azimuth_portion.shape[1]
    ghost_count = 2 * polar_cells + 2 * azimuth_cells
    pair_rows = (polar_cells + azimuth_cells + lon_count - 1) // lon_count
    colatitude_spacing = 0.5 * math.pi / polar_total
    longitude_spacing = 1.5 * math.pi / azimuth_total
    padded_rows = (colat_place * polar_cells + jnp.arange(polar_cells + 2, dtype=jnp.int32)).astype(
        jnp.float32
    )
    colatitude_value = 0.25 * math.pi + (padded_rows - 0.5) * colatitude_spacing
    inner_shell_radius = INNER_RATIO * radial_cells
    row_index = jnp.arange(border_rows, dtype=jnp.int32)
    colat_group = jnp.where(
        row_index < 2 * polar_total,
        row_index % polar_total // polar_cells,
        jnp.where(row_index < 2 * polar_total + azimuth_total, 0, colat_count - 1),
    )
    serving = (source_azimuth_portion[0] == lon_place) & (colat_group == colat_place)
    top_offset = row_index - 2 * polar_total
    target_lon = jnp.where(
        row_index < polar_total,
        0,
        jnp.where(
            row_index < 2 * polar_total, lon_count - 1, top_offset % azimuth_total // azimuth_cells
        ),
    )
    member = serving[:, None] & (
        target_lon[:, None] == jnp.arange(lon_count, dtype=jnp.int32)[None, :]
    )
    running = jnp.cumsum(member.astype(jnp.int32), axis=0)
    slot_rank = jnp.sum(jnp.where(member, running, 0), axis=1) - 1
    slot_total = lon_count * pair_rows
    slot_place = jnp.where(
        serving & (slot_rank < pair_rows), target_lon * pair_rows + slot_rank, slot_total
    )
    slot_ids = jnp.full((slot_total,), -1, jnp.int32).at[slot_place].set(row_index, mode="drop")
    picked = jnp.maximum(slot_ids, 0)
    donor_cells = source_first_slot[0][picked]
    along_polar = source_bilinear_weights[0, 0][picked]
    along_azimuth = source_bilinear_weights[0, 1][picked]
    turn_angle = source_frame_rotation[0][picked]
    fields_now = jnp.concatenate(
        [flow_vector[0], mean_stress[0][None], shear_resistance[0][None]], axis=0
    )
    viscosity_padded = None
    smoothed_flow_vector = flow_vector[0]
    smoothed_mean_stress = mean_stress[0]
    for sweep_index in range(SWEEPS):
        field_count = fields_now.shape[0]
        flattened = fields_now.reshape(field_count, polar_cells * azimuth_cells, radial_cells)
        corner_first = flattened[:, donor_cells]
        corner_east = flattened[:, donor_cells + 1]
        corner_south = flattened[:, donor_cells + azimuth_cells]
        corner_last = flattened[:, donor_cells + azimuth_cells + 1]
        outgoing = blend_rotate(
            corner_first,
            corner_east,
            corner_south,
            corner_last,
            along_polar,
            along_azimuth,
            turn_angle,
        ).transpose(1, 0, 2)
        empty = jnp.zeros((ghost_count, field_count, radial_cells), jnp.float32)
        moved_vals, moved_ids = partner((outgoing, slot_ids), "panel", 0)
        routed_vals = lax.all_to_all(moved_vals, "lon", split_axis=0, concat_axis=0, tiled=True)
        routed_ids = lax.all_to_all(moved_ids, "lon", split_axis=0, concat_axis=0, tiled=True)
        north_offset = routed_ids - 2 * polar_total
        south_offset = north_offset - azimuth_total
        west_side = (routed_ids >= 0) & (routed_ids < polar_total) & (lon_place == 0)
        east_side = (
            (routed_ids >= polar_total)
            & (routed_ids < 2 * polar_total)
            & (lon_place == lon_count - 1)
        )
        north_side = (
            (north_offset >= 0)
            & (north_offset < azimuth_total)
            & (north_offset // azimuth_cells == lon_place)
        )
        south_side = (south_offset >= 0) & (south_offset // azimuth_cells == lon_place)
        ghosts = empty.at[
            jnp.where(
                west_side,
                routed_ids % polar_cells,
                jnp.where(
                    east_side,
                    polar_cells + routed_ids % polar_cells,
                    jnp.where(
                        north_side,
                        2 * polar_cells + north_offset % azimuth_cells,
                        jnp.where(
                            south_side,
                            2 * polar_cells + azimuth_cells + south_offset % azimuth_cells,
                            ghost_count,
                        ),
                    ),
                ),
            )
        ].add(routed_vals, mode="drop")
        assemble_ghosts = ghosts.transpose(1, 0, 2)
        haloed_quantity = extended(fields_now, (("lon", 2), ("colat", 1)), 1)
        haloed_quantity = haloed_quantity.at[:, 1 : polar_cells + 1, 0].add(
            assemble_ghosts[:, :polar_cells]
        )
        haloed_quantity = haloed_quantity.at[:, 1 : polar_cells + 1, azimuth_cells + 1].add(
            assemble_ghosts[:, polar_cells : 2 * polar_cells]
        )
        haloed_quantity = haloed_quantity.at[:, 0, 1 : azimuth_cells + 1].add(
            assemble_ghosts[:, 2 * polar_cells : 2 * polar_cells + azimuth_cells]
        )
        haloed_quantity = haloed_quantity.at[:, polar_cells + 1, 1 : azimuth_cells + 1].add(
            assemble_ghosts[:, 2 * polar_cells + azimuth_cells :]
        )
        if sweep_index == 0:
            viscosity_padded = haloed_quantity[4]
        smoothed_flow_vector, smoothed_mean_stress = weighted_smoothing_pass(
            haloed_quantity[:3],
            haloed_quantity[3],
            viscosity_padded,
            thermal_anomaly[0],
            colatitude_value,
            inner_shell_radius,
            colatitude_spacing,
            longitude_spacing,
        )
        fields_now = jnp.concatenate([smoothed_flow_vector, smoothed_mean_stress[None]], axis=0)
    return (smoothed_flow_vector[None], smoothed_mean_stress[None])


def solution(mesh):
    return jax.shard_map(
        body,
        mesh=mesh,
        in_specs=(
            P("panel", None, "colat", "lon", None),
            P("panel", "colat", "lon", None),
            P("panel", "colat", "lon", None),
            P("panel", "colat", "lon", None),
            P("panel", None),
            P("panel", None),
            P("panel", None, None),
            P("panel", None),
        ),
        out_specs=(P("panel", None, "colat", "lon", None), P("panel", "colat", "lon", None)),
        check_vma=False,
    )
```

profile of v0, /device:TPU:0, one launch (start us, length us, event | category | flops | bytes accessed | tf_op | source)
XLA Modules:
  0.0 92.3 jit_solution(1694525137228731834)
XLA Ops:
  0.7 0.7 compare_reduce_fusion
  1.4 1.1 %reduce-window.6 = s32[8,4,128]{2,0,1:T(8,128)S(1)} reduce-window(s32[8,4,128]{2,0,1:T(8,128)S(1)} %convert_bitcast_fusion, s32[]{:T(128)} %constant.360.clone.1), window={size=1x1x128 pad=0_0x0_0x127_0}, to_apply=%region_0.1 | reduce-window | flops 520192 | bytes 32772 | tf_op jit(solution)/shard_map/reduce-window
  3.0 0.7 compare_select_fusion
  3.7 2.9 %scatter_custom_fusion = s32[32]{0:T(128)S(1)} fusion(s32[416]{0:T(512)S(1)} %bitcast.295, s32[416]{0:T(512)S(1)} %iota.88, s32[]{:T(128)} %constant.355.clone.1), kind=kCustom, calls=%fused_computation.366 | custom fusion | bytes 132 | tf_op jit(solution)/shard_map/scatter | solution.py:201
  6.6 3.0 %collective-permute-start.4 = (s32[32]{0:T(128)S(1)}, s32[32]{0:T(128)S(1)}, u32[]{:S(2)}, u32[]{:S(2)}) collective-permute-start(s32[32]{0:T(128)S(1)} %scatter_custom_fusion), channel_id=1, source_target_pairs={{0,16},{16,0},{1,17},{17,1},{2,18},{18,2},{3,19},{19,3},{4,20},{20... | collective-permute-start | bytes 392 | tf_op jit(solution)/shard_map/ppermute | solution.py:23
  9.6 1.2 %copy.214 = f32[1,3,8,24,128]{4,1,3,2,0:T(4,128)S(1)} copy(f32[1,3,8,24,128]{4,3,2,1,0:T(8,128)} %param.24) | data formatting | bytes 589824 | tf_op args[0]
  10.8 0.8 pad_maximum_fusion.17
  11.6 3.4 %collective-permute-start = (f32[5,8,1,128]{3,0,2,1:T(8,128)S(1)}, f32[5,8,1,128]{3,0,2,1:T(8,128)S(1)}, u32[]{:S(2)}, u32[]{:S(2)}) collective-permute-start(f32[5,8,1,128]{3,0,2,1:T(8,128)S(1)} %get-tuple-element.120), channel_id=1, source_target_pairs={{0,2},{2,4},{4,6},{6,8},{8,10},{10,12},{12,14},{1,3},{3,5},{5,7},{... | collective-permute-start | bytes 61448 | tf_op jit(solution)/shard_map/ppermute | solution.py:34
  15.0 1.3 %collective-permute-start.1 = (f32[5,8,1,128]{3,0,2,1:T(8,128)S(1)}, f32[5,8,1,128]{3,0,2,1:T(8,128)S(1)}, u32[]{:S(2)}, u32[]{:S(2)}) collective-permute-start(f32[5,8,1,128]{3,0,2,1:T(8,128)S(1)} %get-tuple-element.121), channel_id=1, source_target_pairs={{2,0},{4,2},{6,4},{8,6},{10,8},{12,10},{14,12},{3,1},{5,3},{7,5},{... | collective-permute-start | bytes 61448 | tf_op jit(solution)/shard_map/ppermute | solution.py:36
  16.4 0.7 gather_fusion.1
  17.1 0.7 gather_fusion
  17.8 0.7 gather_fusion.7
  18.5 0.7 gather_fusion.2
  19.6 0.6 gather_fusion.6
  20.2 0.6 gather_fusion.5
  20.8 0.6 gather_fusion.4
  21.4 0.6 gather_fusion.3
  22.2 0.6 collective-permute-start.5
  22.9 0.6 fusion.199
  23.7 0.7 all_to_all.15
  24.4 7.0 %all-to-all-start = ((s32[8,4,1]{1,2,0:T(1,128)}), s32[8,4,1]{1,2,0:T(1,128)S(1)}, u32[]{:S(2)}, u32[]{:S(2)}) async-start(s32[8,4,1]{1,2,0:T(1,128)} %bitcast.9), calls=%async_computation | async-start | bytes 8192 | tf_op jit(solution)/shard_map/all_to_all | solution.py:232
  31.4 6.4 %all-to-all-done = s32[8,4,1]{1,2,0:T(1,128)S(1)} async-done(((s32[8,4,1]{1,2,0:T(1,128)}), s32[8,4,1]{1,2,0:T(1,128)S(1)}, u32[]{:S(2)}, u32[]{:S(2)}) %all-to-all-start) | async-done | bytes 160 | tf_op jit(solution)/shard_map/all_to_all | solution.py:232
  38.2 0.7 reduce.23
  39.1 1.3 %collective-permute-start.2 = (f32[5,1,26,128]{3,0,2,1:T(8,128)S(1)}, f32[5,1,26,128]{3,0,2,1:T(8,128)S(1)}, u32[]{:S(2)}, u32[]{:S(2)}) collective-permute-start(f32[5,1,26,128]{3,0,2,1:T(8,128)S(1)} %get-tuple-element.118), channel_id=1, source_target_pairs={{0,1},{2,3},{4,5},{6,7},{8,9},{10,11},{12,13},{14,15},{16,17},{18,... | collective-permute-start | bytes 199688 | tf_op jit(solution)/shard_map/ppermute | solution.py:34
  40.4 1.3 %collective-permute-start.3 = (f32[5,1,26,128]{3,0,2,1:T(8,128)S(1)}, f32[5,1,26,128]{3,0,2,1:T(8,128)S(1)}, u32[]{:S(2)}, u32[]{:S(2)}) collective-permute-start(f32[5,1,26,128]{3,0,2,1:T(8,128)S(1)} %get-tuple-element.119), channel_id=1, source_target_pairs={{1,0},{3,2},{5,4},{7,6},{9,8},{11,10},{13,12},{15,14},{17,16},{19,... | collective-permute-start | bytes 199688 | tf_op jit(solution)/shard_map/ppermute | solution.py:36
  41.7 0.7 copy.126
  42.4 3.4 %all-to-all-start.1 = ((f32[32,5,128]{2,1,0:T(8,128)}), f32[32,5,128]{2,1,0:T(8,128)S(1)}, u32[]{:S(2)}, u32[]{:S(2)}) async-start(f32[32,5,128]{2,1,0:T(8,128)} %copy.126), calls=%async_computation.1 | async-start | bytes 262144 | tf_op jit(solution)/shard_map/all_to_all | solution.py:231
  46.1 7.7 %all-to-all-done.1 = f32[32,5,128]{2,1,0:T(8,128)S(1)} async-done(((f32[32,5,128]{2,1,0:T(8,128)}), f32[32,5,128]{2,1,0:T(8,128)S(1)}, u32[]{:S(2)}, u32[]{:S(2)}) %all-to-all-start.1) | async-done | bytes 81952 | tf_op jit(solution)/shard_map/all_to_all | solution.py:231
  53.8 1.6 %scatter_fusion = f32[64,5,128]{2,1,0:T(8,128)S(1)} fusion(f32[64,5,128]{2,1,0:T(8,128)S(1)} %broadcast_in_dim.31, s32[32]{0:T(128)S(1)} %fusion.164, f32[32,5,128]{2,1,0:T(8,128)S(1)} %all-to-all-done.1), kind=kCustom, calls=%fused_computation.13 | custom fusion | flops 20480 | bytes 245888 | tf_op jit(solution)/shard_map/scatter-add | solution.py:265
  55.5 1.2 %fusion.109 = f32[5,10,26,128]{3,0,2,1:T(8,128)S(1)} fusion(f32[5,10,26,128]{3,0,2,1:T(8,128)S(1)} %fusion.127, s32[]{:T(128)} %bitcast.28, s32[]{:T(128)} %bitcast.29, f32[5,64,128]{2,0,1:T(8,128)S(1)} %bitcast.277), kind=kLoop, calls=%fused_computation.184 | loop fusion | flops 15360 | bytes 294920 | tf_op jit(solution)/shard_map/scatter-add | solution.py:274
  59.9 0.6 gather_fusion.11
  60.5 0.6 gather_fusion.10
  61.2 0.6 gather_fusion.9
  61.8 0.6 gather_fusion.8
  62.4 1.8 %collective-permute-start.6 = (f32[4,8,1,128]{3,1,0,2:T(8,128)S(1)}, f32[4,8,1,128]{3,1,0,2:T(8,128)S(1)}, u32[]{:S(2)}, u32[]{:S(2)}) collective-permute-start(f32[4,8,1,128]{3,1,0,2:T(8,128)S(1)} %bitcast.293), channel_id=1, source_target_pairs={{0,2},{2,4},{4,6},{6,8},{8,10},{10,12},{12,14},{1,3},{3,5},{5,7},{... | collective-permute-start | bytes 49160 | tf_op jit(solution)/shard_map/ppermute | solution.py:34
  64.2 1.3 %collective-permute-start.7 = (f32[4,8,1,128]{3,2,1,0:T(1,128)S(1)}, f32[4,8,1,128]{3,2,1,0:T(1,128)S(1)}, u32[]{:S(2)}, u32[]{:S(2)}) collective-permute-start(f32[4,8,1,128]{3,2,1,0:T(1,128)S(1)} %get-tuple-element.125), channel_id=1, source_target_pairs={{2,0},{4,2},{6,4},{8,6},{10,8},{12,10},{14,12},{3,1},{5,3},{7,5},{... | collective-permute-start | bytes 49160 | tf_op jit(solution)/shard_map/ppermute | solution.py:36
  65.7 1.6 %collective-permute-start.10 = (f32[32,4,128]{2,0,1:T(8,128)S(1)}, f32[32,4,128]{2,0,1:T(8,128)S(1)}, u32[]{:S(2)}, u32[]{:S(2)}) collective-permute-start(f32[32,4,128]{2,0,1:T(8,128)S(1)} %maximum_bitcast_fusion.2), channel_id=1, source_target_pairs={{0,16},{16,0},{1,17},{17,1},{2,18},{18,2},{3,19},{19,3},{4,20},{20... | collective-permute-start | bytes 196616 | tf_op jit(solution)/shard_map/ppermute | solution.py:23
  67.2 2.6 %collective-permute-done.7 = f32[4,8,1,128]{3,2,1,0:T(1,128)S(1)} collective-permute-done((f32[4,8,1,128]{3,2,1,0:T(1,128)S(1)}, f32[4,8,1,128]{3,2,1,0:T(1,128)S(1)}, u32[]{:S(2)}, u32[]{:S(2)}) %collective-permute-start.7) | collective-permute-done | bytes 16416 | tf_op jit(solution)/shard_map/ppermute | solution.py:36
  69.9 1.3 %collective-permute-start.8 = (f32[4,1,26,128]{3,2,1,0:T(8,128)S(1)}, f32[4,1,26,128]{3,2,1,0:T(8,128)S(1)}, u32[]{:S(2)}, u32[]{:S(2)}) collective-permute-start(f32[4,1,26,128]{3,2,1,0:T(8,128)S(1)} %get-tuple-element.122), channel_id=1, source_target_pairs={{0,1},{2,3},{4,5},{6,7},{8,9},{10,11},{12,13},{14,15},{16,17},{18,... | collective-permute-start | bytes 159752 | tf_op jit(solution)/shard_map/ppermute | solution.py:34
  71.2 1.3 %collective-permute-start.9 = (f32[4,1,26,128]{3,2,1,0:T(8,128)S(1)}, f32[4,1,26,128]{3,2,1,0:T(8,128)S(1)}, u32[]{:S(2)}, u32[]{:S(2)}) collective-permute-start(f32[4,1,26,128]{3,2,1,0:T(8,128)S(1)} %get-tuple-element.123), channel_id=1, source_target_pairs={{1,0},{3,2},{5,4},{7,6},{9,8},{11,10},{13,12},{15,14},{17,16},{19,... | collective-permute-start | bytes 159752 | tf_op jit(solution)/shard_map/ppermute | solution.py:36
  72.5 0.7 copy.146
  73.1 4.4 %all-to-all-start.2 = ((f32[32,4,128]{2,1,0:T(4,128)}), f32[32,4,128]{2,1,0:T(4,128)S(1)}, u32[]{:S(2)}, u32[]{:S(2)}) async-start(f32[32,4,128]{2,1,0:T(4,128)} %copy.146), calls=%async_computation.2 | async-start | bytes 131072 | tf_op jit(solution)/shard_map/all_to_all | solution.py:231
  77.7 7.2 %all-to-all-done.2 = f32[32,4,128]{2,1,0:T(4,128)S(1)} async-done(((f32[32,4,128]{2,1,0:T(4,128)}), f32[32,4,128]{2,1,0:T(4,128)S(1)}, u32[]{:S(2)}, u32[]{:S(2)}) %all-to-all-start.2) | async-done | bytes 65568 | tf_op jit(solution)/shard_map/all_to_all | solution.py:231
  84.9 1.6 %scatter_fusion.1 = f32[64,4,128]{2,1,0:T(4,128)S(1)} fusion(f32[64,4,128]{2,1,0:T(4,128)S(1)} %broadcast_in_dim.38, s32[32]{0:T(128)S(1)} %fusion.164, f32[32,4,128]{2,1,0:T(4,128)S(1)} %all-to-all-done.2), kind=kCustom, calls=%fused_computation.14 | custom fusion | flops 16384 | bytes 196736 | tf_op jit(solution)/shard_map/scatter-add | solution.py:265
  86.8 1.2 %fusion.125 = f32[4,1,24,128]{3,2,1,0:T(8,128)S(1)} fusion(f32[4,64,128]{2,1,0:T(8,128)S(1)} %bitcast.282, f32[4,10,26,128]{3,2,1,0:T(8,128)S(1)} %scatter-add.61, s32[]{:T(128)} %bitcast.28, s32[]{:T(128)} %bitcast.29), kind=kLoop, calls=%fused_computation.223 | loop fusion | flops 12288 | bytes 147464 | tf_op jit(solution)/shard_map/add | solution.py:274
  88.1 1.4 %scatter-add.62 = f32[4,10,26,128]{3,2,1,0:T(8,128)S(1)} dynamic-update-slice(f32[4,10,26,128]{3,2,1,0:T(8,128)S(1)} %scatter-add.61, f32[4,1,24,128]{3,2,1,0:T(8,128)S(1)} %fusion.125, s32[]{:T(128)} %constant.360.clone.1, s32[]{:T(128)} %bitcast.28, s32[]{:T(128)} %bitcast.29, s32[]{:T(128)} %constant.360.clone.1) | dynamic-update-slice | bytes 98308 | tf_op jit(solution)/shard_map/scatter-add | solution.py:274
  90.3 0.8 fusion.6
  91.6 0.7 maximum_bitcast_fusion
  (109 shorter events, 7.2 us)
Async XLA Ops:
  0.6 17.2 %copy-start = (f32[1,416]{1,0:T(1,128)S(1)}, f32[1,416]{1,0:T(1,128)}, u32[]{:S(2)}) copy-start(f32[1,416]{1,0:T(1,128)} %param.31) | copy-start | bytes 4996
  0.6 15.7 %copy-start.5 = (f32[1,2,416]{2,1,0:T(2,128)S(1)}, f32[1,2,416]{2,1,0:T(2,128)}, u32[]{:S(2)}) copy-start(f32[1,2,416]{2,1,0:T(2,128)} %param.30) | copy-start | bytes 9988
  6.6 17.1 %collective-permute-start.4 = (s32[32]{0:T(128)S(1)}, s32[32]{0:T(128)S(1)}, u32[]{:S(2)}, u32[]{:S(2)}) collective-permute-start(s32[32]{0:T(128)S(1)} %scatter_custom_fusion), channel_id=1, source_target_pairs={{0,16},{16,0},{1,17},{17,1},{2,18},{18,2},{3,19},{19,3},{4,20},{20... | collective-permute-start | bytes 392 | tf_op jit(solution)/shard_map/ppermute | solution.py:23
  10.8 7.7 %copy-start.1 = (s32[1,416]{1,0:T(1,128)S(1)}, s32[1,416]{1,0:T(1,128)}, u32[]{:S(2)}) copy-start(s32[1,416]{1,0:T(1,128)} %param.29) | copy-start | bytes 4996
  11.6 27.4 %collective-permute-start = (f32[5,8,1,128]{3,0,2,1:T(8,128)S(1)}, f32[5,8,1,128]{3,0,2,1:T(8,128)S(1)}, u32[]{:S(2)}, u32[]{:S(2)}) collective-permute-start(f32[5,8,1,128]{3,0,2,1:T(8,128)S(1)} %get-tuple-element.120), channel_id=1, source_target_pairs={{0,2},{2,4},{4,6},{6,8},{8,10},{10,12},{12,14},{1,3},{3,5},{5,7},{... | collective-permute-start | bytes 61448 | tf_op jit(solution)/shard_map/ppermute | solution.py:34
  15.0 24.0 %collective-permute-start.1 = (f32[5,8,1,128]{3,0,2,1:T(8,128)S(1)}, f32[5,8,1,128]{3,0,2,1:T(8,128)S(1)}, u32[]{:S(2)}, u32[]{:S(2)}) collective-permute-start(f32[5,8,1,128]{3,0,2,1:T(8,128)S(1)} %get-tuple-element.121), channel_id=1, source_target_pairs={{2,0},{4,2},{6,4},{8,6},{10,8},{12,10},{14,12},{3,1},{5,3},{7,5},{... | collective-permute-start | bytes 61448 | tf_op jit(solution)/shard_map/ppermute | solution.py:36
  16.3 3.0 %copy-start.2 = (f32[1,8,24,128]{3,2,1,0:T(8,128)S(1)}, f32[1,8,24,128]{3,2,1,0:T(8,128)}, u32[]{:S(2)}) copy-start(f32[1,8,24,128]{3,2,1,0:T(8,128)} %param.26) | copy-start | bytes 294916
  16.4 3.0 %copy-start.3 = (f32[1,8,24,128]{3,2,1,0:T(8,128)S(1)}, f32[1,8,24,128]{3,2,1,0:T(8,128)}, u32[]{:S(2)}) copy-start(f32[1,8,24,128]{3,2,1,0:T(8,128)} %param.25) | copy-start | bytes 294916
  22.2 19.5 %collective-permute-start.5 = (f32[32,5,128]{2,0,1:T(8,128)S(1)}, f32[32,5,128]{2,0,1:T(8,128)S(1)}, u32[]{:S(2)}, u32[]{:S(2)}) collective-permute-start(f32[32,5,128]{2,0,1:T(8,128)S(1)} %maximum_bitcast_fusion.1), channel_id=1, source_target_pairs={{0,16},{16,0},{1,17},{17,1},{2,18},{18,2},{3,19},{19,3},{4,20},{20... | collective-permute-start | bytes 245768 | tf_op jit(solution)/shard_map/ppermute | solution.py:23
  24.4 13.3 %all-to-all-start = ((s32[8,4,1]{1,2,0:T(1,128)}), s32[8,4,1]{1,2,0:T(1,128)S(1)}, u32[]{:S(2)}, u32[]{:S(2)}) async-start(s32[8,4,1]{1,2,0:T(1,128)} %bitcast.9), calls=%async_computation | async-start | bytes 8192 | tf_op jit(solution)/shard_map/all_to_all | solution.py:232
  39.1 6.7 %collective-permute-start.2 = (f32[5,1,26,128]{3,0,2,1:T(8,128)S(1)}, f32[5,1,26,128]{3,0,2,1:T(8,128)S(1)}, u32[]{:S(2)}, u32[]{:S(2)}) collective-permute-start(f32[5,1,26,128]{3,0,2,1:T(8,128)S(1)} %get-tuple-element.118), channel_id=1, source_target_pairs={{0,1},{2,3},{4,5},{6,7},{8,9},{10,11},{12,13},{14,15},{16,17},{18,... | collective-permute-start | bytes 199688 | tf_op jit(solution)/shard_map/ppermute | solution.py:34
  40.4 5.4 %collective-permute-start.3 = (f32[5,1,26,128]{3,0,2,1:T(8,128)S(1)}, f32[5,1,26,128]{3,0,2,1:T(8,128)S(1)}, u32[]{:S(2)}, u32[]{:S(2)}) collective-permute-start(f32[5,1,26,128]{3,0,2,1:T(8,128)S(1)} %get-tuple-element.119), channel_id=1, source_target_pairs={{1,0},{3,2},{5,4},{7,6},{9,8},{11,10},{13,12},{15,14},{17,16},{19,... | collective-permute-start | bytes 199688 | tf_op jit(solution)/shard_map/ppermute | solution.py:36
  42.4 11.4 %all-to-all-start.1 = ((f32[32,5,128]{2,1,0:T(8,128)}), f32[32,5,128]{2,1,0:T(8,128)S(1)}, u32[]{:S(2)}, u32[]{:S(2)}) async-start(f32[32,5,128]{2,1,0:T(8,128)} %copy.126), calls=%async_computation.1 | async-start | bytes 262144 | tf_op jit(solution)/shard_map/all_to_all | solution.py:231
  57.9 0.9 copy-start.4
  62.4 4.8 %collective-permute-start.6 = (f32[4,8,1,128]{3,1,0,2:T(8,128)S(1)}, f32[4,8,1,128]{3,1,0,2:T(8,128)S(1)}, u32[]{:S(2)}, u32[]{:S(2)}) collective-permute-start(f32[4,8,1,128]{3,1,0,2:T(8,128)S(1)} %bitcast.293), channel_id=1, source_target_pairs={{0,2},{2,4},{4,6},{6,8},{8,10},{10,12},{12,14},{1,3},{3,5},{5,7},{... | collective-permute-start | bytes 49160 | tf_op jit(solution)/shard_map/ppermute | solution.py:34
  64.2 5.6 %collective-permute-start.7 = (f32[4,8,1,128]{3,2,1,0:T(1,128)S(1)}, f32[4,8,1,128]{3,2,1,0:T(1,128)S(1)}, u32[]{:S(2)}, u32[]{:S(2)}) collective-permute-start(f32[4,8,1,128]{3,2,1,0:T(1,128)S(1)} %get-tuple-element.125), channel_id=1, source_target_pairs={{2,0},{4,2},{6,4},{8,6},{10,8},{12,10},{14,12},{3,1},{5,3},{7,5},{... | collective-permute-start | bytes 49160 | tf_op jit(solution)/shard_map/ppermute | solution.py:36
  65.7 6.8 %collective-permute-start.10 = (f32[32,4,128]{2,0,1:T(8,128)S(1)}, f32[32,4,128]{2,0,1:T(8,128)S(1)}, u32[]{:S(2)}, u32[]{:S(2)}) collective-permute-start(f32[32,4,128]{2,0,1:T(8,128)S(1)} %maximum_bitcast_fusion.2), channel_id=1, source_target_pairs={{0,16},{16,0},{1,17},{17,1},{2,18},{18,2},{3,19},{19,3},{4,20},{20... | collective-permute-start | bytes 196616 | tf_op jit(solution)/shard_map/ppermute | solution.py:23
  69.9 7.7 %collective-permute-start.8 = (f32[4,1,26,128]{3,2,1,0:T(8,128)S(1)}, f32[4,1,26,128]{3,2,1,0:T(8,128)S(1)}, u32[]{:S(2)}, u32[]{:S(2)}) collective-permute-start(f32[4,1,26,128]{3,2,1,0:T(8,128)S(1)} %get-tuple-element.122), channel_id=1, source_target_pairs={{0,1},{2,3},{4,5},{6,7},{8,9},{10,11},{12,13},{14,15},{16,17},{18,... | collective-permute-start | bytes 159752 | tf_op jit(solution)/shard_map/ppermute | solution.py:34
  71.2 6.4 %collective-permute-start.9 = (f32[4,1,26,128]{3,2,1,0:T(8,128)S(1)}, f32[4,1,26,128]{3,2,1,0:T(8,128)S(1)}, u32[]{:S(2)}, u32[]{:S(2)}) collective-permute-start(f32[4,1,26,128]{3,2,1,0:T(8,128)S(1)} %get-tuple-element.123), channel_id=1, source_target_pairs={{1,0},{3,2},{5,4},{7,6},{9,8},{11,10},{13,12},{15,14},{17,16},{19,... | collective-permute-start | bytes 159752 | tf_op jit(solution)/shard_map/ppermute | solution.py:36
  73.1 11.7 %all-to-all-start.2 = ((f32[32,4,128]{2,1,0:T(4,128)}), f32[32,4,128]{2,1,0:T(4,128)S(1)}, u32[]{:S(2)}, u32[]{:S(2)}) async-start(f32[32,4,128]{2,1,0:T(4,128)} %copy.146), calls=%async_computation.2 | async-start | bytes 131072 | tf_op jit(solution)/shard_map/all_to_all | solution.py:231
where the time goes:
time: 93 us; the launch traced here: 92.3 us
  starting transfers between devices  32.9 us (35%)
  waiting for transfers between devices  23.8 us (26%)
  local copies, waits for them, and re-layouts  19.3 us (21%)
  other arithmetic  14.9 us (16%)
  between operations  1.4 us (2%)
    all_to_all x2, waiting for transfers between devices, body(): lax.all_to_all(moved_vals, 'lon', split_axis=0, concat_axis=0, tiled=True)  14.9 us
    ppermute x4, starting transfers between devices, extended(): lax.ppermute(tail, axis, [(i, (i + 1) % count) for i in range(ends)])  7.81 us
    all_to_all x2, starting transfers between devices, body(): lax.all_to_all(moved_vals, 'lon', split_axis=0, concat_axis=0, tiled=True)  7.81 us
    all_to_all x1, starting transfers between devices, body(): lax.all_to_all(moved_ids, 'lon', split_axis=0, concat_axis=0, tiled=True)  6.96 us
    all_to_all x1, waiting for transfers between devices, body(): lax.all_to_all(moved_ids, 'lon', split_axis=0, concat_axis=0, tiled=True)  6.37 us
    ppermute x4, starting transfers between devices, extended(): lax.ppermute(head, axis, [((i + 1) % count, i) for i in range(ends)])  5.17 us
    ppermute x3, starting transfers between devices, partner(): return lax.ppermute(block, axis, route)  5.16 us
    scatter-add x2, other arithmetic, body(): ghosts = empty.at[jnp.where(west_side, routed_ids % polar_cells, jnp.wher...  3.27 us
  transfers between devices with their start and end apart: 14, of which 4 were waited for; matrix products, arithmetic and copies ran while one was open for 13% of the time, Pallas kernels for 0%

commit v1 on v0

v1 whole, which is shorter than its diff:
```python
import functools
import math

import jax
import jax.numpy as jnp
import numpy as np
from jax import lax
from jax.experimental import pallas as pl
from jax.experimental.pallas import tpu as pltpu
from jax.sharding import PartitionSpec as P

OMEGA_VELOCITY = 0.8
OMEGA_PRESSURE = 0.1
INNER_RATIO = 11.0 / 9.0
LEFT = 8
HIGHEST = lax.Precision.HIGHEST
SCALARS = 8


def row_constants(tc, ac, lon, colat):
    pt, at = tc * colat, ac * lon
    rows = np.arange(2 * pt + 2 * at)
    side = rows < 2 * pt
    off = rows - 2 * pt
    group = np.where(side, rows % pt // tc, np.where(off < at, 0, colat - 1))
    target = np.where(rows < pt, 0, np.where(side, lon - 1, off % at // ac))
    place = np.where(side, rows % tc, tc + off % at % ac)
    return np.stack([target, group, place + 1]).astype(np.int32)


def polar_constants(tc, ac, lon, colat):
    pt, at = tc * colat, ac * lon
    dth, dph = 0.5 * math.pi / pt, 1.5 * math.pi / at
    th = 0.25 * math.pi + (np.arange(pt, dtype=np.float64) + 0.5) * dth
    s = np.sin(th)
    table = np.zeros((pt, SCALARS))
    table[:, 0] = 0.5 * np.sin(th - 0.5 * dth) / s / dth**2
    table[:, 1] = 0.5 * np.sin(th + 0.5 * dth) / s / dth**2
    table[:, 2] = 0.5 / (s * dph) ** 2
    table[:, 3] = 0.5 / dth
    table[:, 4] = 0.5 / (s * dph)
    table[:, 5] = np.sin(th - dth) / (2 * dth * s)
    table[:, 6] = np.sin(th + dth) / (2 * dth * s)
    return table.reshape(-1).astype(np.float32)


def kernel(
    dims,
    polar_ref,
    const_ref,
    portion_ref,
    slot_ref,
    weight_ref,
    angle_ref,
    flow_hbm,
    pres_hbm,
    visc_hbm,
    heat_hbm,
    vel_out,
    pres_out,
    pad1,
    pad2,
    heat,
    coef,
    lon_send,
    lon_recv,
    send1,
    send2,
    recv1,
    recv2,
    in_sem,
    lon_ssem,
    lon_rsem,
    col_ssem,
    col_rsem,
    pan_ssem,
    pan_rsem,
):
    tc, ac, nk, lon, colat, slots, pack = dims
    rows = const_ref.shape[1]
    cells = tc * ac
    ghosts = tc + ac
    packed = 8 * lon
    p = lax.axis_index("panel")
    l = lax.axis_index("lon")
    c = lax.axis_index("colat")
    other = 1 - p
    inner = pl.ds(LEFT, ac)
    pads, sends, recvs, counts = (pad1, pad2), (send1, send2), (recv1, recv2), (5, 4)

    local = [
        pltpu.make_async_copy(flow_hbm.at[0], pad1.at[0:3, 1 : tc + 1, inner, :], in_sem.at[0]),
        pltpu.make_async_copy(pres_hbm.at[0], pad1.at[3, 1 : tc + 1, inner, :], in_sem.at[1]),
        pltpu.make_async_copy(visc_hbm.at[0], pad1.at[4, 1 : tc + 1, inner, :], in_sem.at[2]),
        pltpu.make_async_copy(heat_hbm.at[0], heat, in_sem.at[3]),
    ]
    for copy in local:
        copy.start()

    barrier = pltpu.get_barrier_semaphore()

    def greet(**where):
        pl.semaphore_signal(
            barrier, inc=1, device_id=where, device_id_type=pl.DeviceIdType.MESH
        )

    def greet_panel(k, carry):
        greet(panel=other, lon=lax.rem(l + k, lon))
        return carry

    lax.fori_loop(0, lon, greet_panel, 0)
    has = {"w": l > 0, "e": l < lon - 1, "n": c > 0, "s": c < colat - 1}
    pl.when(has["w"])(lambda: greet(lon=l - 1))
    pl.when(has["e"])(lambda: greet(lon=l + 1))
    pl.when(has["n"])(lambda: greet(colat=c - 1))
    pl.when(has["s"])(lambda: greet(colat=c + 1))

    target = const_ref[0:1, :]
    serving = (portion_ref[...] == l) & (const_ref[1:2, :] == c)
    wanted = jnp.where(serving, target, -1)
    lon_iota = lax.broadcasted_iota(jnp.int32, (lon, rows), 0)
    member = wanted == lon_iota
    member_f = member.astype(jnp.float32)
    before = (
        lax.broadcasted_iota(jnp.int32, (rows, rows), 0)
        < lax.broadcasted_iota(jnp.int32, (rows, rows), 1)
    ).astype(jnp.float32)
    running = jnp.dot(
        member_f.astype(jnp.bfloat16),
        before.astype(jnp.bfloat16),
        preferred_element_type=jnp.float32,
    )
    rank = jnp.sum(jnp.where(member, running, 0.0), axis=0, keepdims=True)
    key = jnp.where(serving, target.astype(jnp.float32) * slots + rank, -1.0)
    key = jnp.where(rank < slots, key, -1.0)
    line = lax.broadcasted_iota(jnp.int32, (packed, rows), 0)
    line_key = (line >> 3) * slots + (line & (slots - 1))
    chosen = key == line_key.astype(jnp.float32)

    def picked(values):
        return jnp.sum(jnp.where(chosen, values, 0.0), axis=1, keepdims=True)

    angle = angle_ref[...]
    donor = picked(slot_ref[...].astype(jnp.float32))
    frac_t = picked(weight_ref[0, 0:1, :])
    frac_j = picked(weight_ref[0, 1:2, :])
    cosine = picked(jnp.cos(angle))
    sine = picked(jnp.sin(angle))
    ghost_id = picked(const_ref[2:3, :].astype(jnp.float32))
    used = jnp.where(ghost_id > 0.5, 1.0, 0.0)
    step = lax.broadcasted_iota(jnp.int32, (packed, cells), 1).astype(jnp.float32) - donor
    keep_t = (1.0 - frac_t) * used
    lean_t = frac_t * used
    blend = jnp.where(step == 0.0, keep_t * (1.0 - frac_j), 0.0)
    blend = jnp.where(step == 1.0, keep_t * frac_j, blend)
    blend = jnp.where(step == float(ac), lean_t * (1.0 - frac_j), blend)
    blend = jnp.where(step == float(ac + 1), lean_t * frac_j, blend)
    block_of = (
        (lax.broadcasted_iota(jnp.int32, (packed, nk), 0) & 7) >> (slots.bit_length() - 1)
    )

    def lon_copy(sweep, side):
        n = counts[sweep]
        return pltpu.make_async_remote_copy(
            src_ref=lon_send.at[sweep, side, 0:n],
            dst_ref=lon_recv.at[sweep, side, 0:n],
            send_sem=lon_ssem.at[sweep, side],
            recv_sem=lon_rsem.at[sweep, side],
            device_id={"lon": jnp.maximum(l - 1, 0) if side == 0 else jnp.minimum(l + 1, lon - 1)},
            device_id_type=pl.DeviceIdType.MESH,
        )

    def colat_copy(sweep, side):
        pad = pads[sweep]
        from_row, to_row = (1, tc + 1) if side == 0 else (tc, 0)
        return pltpu.make_async_remote_copy(
            src_ref=pad.at[:, from_row, inner, :],
            dst_ref=pad.at[:, to_row, inner, :],
            send_sem=col_ssem.at[sweep, side],
            recv_sem=col_rsem.at[sweep, side],
            device_id={"colat": jnp.maximum(c - 1, 0) if side == 0 else jnp.minimum(c + 1, colat - 1)},
            device_id_type=pl.DeviceIdType.MESH,
        )

    def panel_copy(sweep, to, slot):
        return pltpu.make_async_remote_copy(
            src_ref=sends[sweep].at[to],
            dst_ref=recvs[sweep].at[slot],
            send_sem=pan_ssem.at[sweep, to],
            recv_sem=pan_rsem.at[sweep, slot],
            device_id={"panel": other, "lon": to},
            device_id_type=pl.DeviceIdType.MESH,
        )

    def stage_lon(sweep):
        pad = pads[sweep]
        for f in range(counts[sweep]):
            lon_send[sweep, 0, f] = pad[f, 1 : tc + 1, LEFT, :]
            lon_send[sweep, 1, f] = pad[f, 1 : tc + 1, LEFT + ac - 1, :]

    def start_halos(sweep):
        pl.when(has["n"])(lambda: colat_copy(sweep, 0).start())
        pl.when(has["s"])(lambda: colat_copy(sweep, 1).start())
        pl.when(has["w"])(lambda: lon_copy(sweep, 0).start())
        pl.when(has["e"])(lambda: lon_copy(sweep, 1).start())

    def gather(sweep):
        pad, send, n = pads[sweep], sends[sweep], counts[sweep]
        fields = [
            jnp.dot(
                blend,
                pad[f, 1 : tc + 1, inner, :].reshape(cells, nk),
                precision=HIGHEST,
                preferred_element_type=jnp.float32,
            )
            for f in range(n)
        ]
        polar, azimuth = fields[1], fields[2]
        fields[1] = cosine * polar + sine * azimuth
        fields[2] = cosine * azimuth - sine * polar
        if sweep == 0:
            fields.append(jnp.broadcast_to(ghost_id, (packed, nk)))
        for m in range(send.shape[1]):
            tile = jnp.zeros((packed, nk), jnp.float32)
            for h in range(pack):
                if m * pack + h < len(fields):
                    tile = jnp.where(block_of == h, fields[m * pack + h], tile)
            send[:, m] = tile.reshape(lon, 8, nk)

    def start_panel(sweep):
        def one(k, carry):
            panel_copy(sweep, lax.rem(l + k, lon), l).start()
            return carry

        lax.fori_loop(0, lon, one, 0)

    def wait_all(sweep):
        pl.when(has["e"])(lambda: lon_copy(sweep, 0).wait_recv())
        pl.when(has["w"])(lambda: lon_copy(sweep, 1).wait_recv())
        pl.when(has["s"])(lambda: colat_copy(sweep, 0).wait_recv())
        pl.when(has["n"])(lambda: colat_copy(sweep, 1).wait_recv())

        def one(k, carry):
            panel_copy(sweep, k, k).wait_recv()
            return carry

        lax.fori_loop(0, lon, one, 0)

    def wait_sent(sweep):
        pl.when(has["n"])(lambda: colat_copy(sweep, 0).wait_send())
        pl.when(has["s"])(lambda: colat_copy(sweep, 1).wait_send())
        pl.when(has["w"])(lambda: lon_copy(sweep, 0).wait_send())
        pl.when(has["e"])(lambda: lon_copy(sweep, 1).wait_send())

        def one(k, carry):
            panel_copy(sweep, k, l).wait_send()
            return carry

        lax.fori_loop(0, lon, one, 0)

    def placing():
        m, h = 5 // pack, 5 % pack
        tile = recv1[:, m].reshape(packed, nk)
        ids = jnp.where(block_of == h, tile, 0.0).reshape(lon, 8, nk)
        total = ids
        for turn in range(1, pack):
            total = total + pltpu.roll(ids, turn * slots, 1)
        total = total.reshape(packed, nk)
        blocks = []
        for h in range(pack):
            place = lax.broadcasted_iota(jnp.int32, (packed, ghosts), 1).astype(jnp.float32) + 1.0
            hit = (total[:, :ghosts] == place) & (block_of[:, :ghosts] == h)
            blocks.append(jnp.where(hit, 1.0, 0.0))
        return jnp.concatenate(blocks, axis=1)

    def assemble(sweep, where_to):
        pad, recv, n = pads[sweep], recvs[sweep], counts[sweep]
        for m in range(recv.shape[1]):
            if m * pack >= n:
                continue
            placed = lax.dot_general(
                where_to,
                recv[:, m].reshape(packed, nk),
                (((0,), (0,)), ((), ())),
                precision=HIGHEST,
                preferred_element_type=jnp.float32,
            )
            for h in range(pack):
                f = m * pack + h
                if f >= n:
                    continue
                mine = placed[h * ghosts : (h + 1) * ghosts]
                side, band = mine[:tc], mine[tc:]
                pad[f, 1 : tc + 1, LEFT - 1, :] = jnp.where(has["w"], lon_recv[sweep, 1, f], side)
                pad[f, 1 : tc + 1, LEFT + ac, :] = jnp.where(has["e"], lon_recv[sweep, 0, f], side)

                @pl.when(c == 0)
                def _():
                    pad[f, 0, inner, :] = band

                @pl.when(c == colat - 1)
                def _():
                    pad[f, tc + 1, inner, :] = band

    lane = lax.broadcasted_iota(jnp.int32, (1, nk), 1)
    radius = INNER_RATIO * nk + lane.astype(jnp.float32) + 0.5
    inv = 1.0 / radius
    inv2 = inv * inv
    top, bottom = lane == nk - 1, lane == 0
    up_geo = 0.5 * ((radius + 0.5) * inv) ** 2
    down_geo = 0.5 * ((radius - 0.5) * inv) ** 2
    grad_up = jnp.where(top, 0.0, 0.5)
    grad_down = jnp.where(bottom, 0.0, 0.5)
    div_up = jnp.where(top, 0.0, 0.5 * ((radius + 1.0) * inv) ** 2)
    div_down = jnp.where(bottom, 0.0, 0.5 * ((radius - 1.0) * inv) ** 2)

    def above(x):
        return pltpu.roll(x, nk - 1, 1)

    def below(x):
        return pltpu.roll(x, 1, 1)

    def smooth(sweep):
        pad = pads[sweep]

        def row(t, carry):
            scalar = lambda i: polar_ref[(c * tc + t) * SCALARS + i]

            def near(f):
                return (
                    pad[f, t + 1, inner, :],
                    pad[f, t, inner, :],
                    pad[f, t + 2, inner, :],
                    pad[f, t + 1, pl.ds(LEFT - 1, ac), :],
                    pad[f, t + 1, pl.ds(LEFT + 1, ac), :],
                )

            if sweep == 0:
                e, en, es, ew, ee = near(4)
                e_up = jnp.where(top, e, above(e))
                e_dn = jnp.where(bottom, e, below(e))
                a_up = (e + e_up) * up_geo
                a_dn = (e + e_dn) * down_geo
                a_n = (e + en) * (scalar(0) * inv2)
                a_s = (e + es) * (scalar(1) * inv2)
                h2 = scalar(2) * inv2
                a_w = (e + ew) * h2
                a_e = (e + ee) * h2
                d = OMEGA_VELOCITY / (a_up + a_dn + a_n + a_s + a_w + a_e)
                b_up = jnp.where(top, 0.0, a_up * d)
                b_dn = jnp.where(bottom, 0.0, a_dn * d)
                b_n, b_s, b_w, b_e = a_n * d, a_s * d, a_w * d, a_e * d
                for i, b in enumerate((b_up, b_dn, b_n, b_s, b_w, b_e, d)):
                    coef[i, t] = b
            else:
                b_up, b_dn, b_n, b_s, b_w, b_e, d = [coef[i, t] for i in range(7)]
                e = pad1[4, t + 1, inner, :]
            pc, pn, ps, pw, pe = near(3)
            az = scalar(4) * inv
            forcing = (
                heat[t] - (grad_up * above(pc) - grad_down * below(pc)),
                (pn - ps) * (scalar(3) * inv),
                (pw - pe) * az,
            )
            new = []
            div = None
            for f in range(3):
                w, wn, ws, ww, we = near(f)
                wu, wd = above(w), below(w)
                total = b_up * wu + b_dn * wd + b_n * wn + b_s * ws + b_w * ww + b_e * we
                new.append((1.0 - OMEGA_VELOCITY) * w + (total + d * forcing[f]))
                if f == 0:
                    div = div_up * wu - div_down * wd
                elif f == 1:
                    div = div + (scalar(6) * ws - scalar(5) * wn) * inv
                else:
                    div = div + (we - ww) * az
            new.append(pc - OMEGA_PRESSURE * e * div)
            if sweep == 0:
                for f in range(4):
                    pad2[f, t + 1, inner, :] = new[f]
            else:
                for f in range(3):
                    vel_out[0, f, t] = new[f]
                pres_out[0, t] = new[3]
            return carry

        lax.fori_loop(0, tc, row, 0)

    greeted = lon + sum(has[side].astype(jnp.int32) for side in "wens")
    for copy in local:
        copy.wait()
    gather(0)
    stage_lon(0)
    pl.semaphore_wait(barrier, greeted)
    start_panel(0)
    start_halos(0)
    wait_all(0)
    where_to = placing()
    assemble(0, where_to)
    smooth(0)
    stage_lon(1)
    start_halos(1)
    gather(1)
    start_panel(1)
    wait_all(1)
    assemble(1, where_to)
    smooth(1)
    wait_sent(0)
    wait_sent(1)


def body(lon, colat, flow, pres, visc, heat, portion, slot, weights, angle):
    tc, ac, nk = flow.shape[2:]
    rows = portion.shape[1]
    pair_rows = (tc + ac + lon - 1) // lon
    slots = 1
    while slots < pair_rows:
        slots *= 2
    pack = 8 // slots
    tiles1, tiles2 = -(-6 // pack), -(-4 // pack)
    f32 = jnp.float32
    vmem = pl.BlockSpec(memory_space=pltpu.VMEM)
    hbm = pl.BlockSpec(memory_space=pl.ANY)
    smem = pl.BlockSpec(memory_space=pltpu.SMEM)
    wide = LEFT + ac + 8
    return pl.pallas_call(
        functools.partial(kernel, (tc, ac, nk, lon, colat, slots, pack)),
        out_shape=(jax.ShapeDtypeStruct(flow.shape, f32), jax.ShapeDtypeStruct(pres.shape, f32)),
        in_specs=[smem] + [vmem] * 5 + [hbm] * 4,
        out_specs=(vmem, vmem),
        scratch_shapes=[
            pltpu.VMEM((5, tc + 2, wide, nk), f32),
            pltpu.VMEM((4, tc + 2, wide, nk), f32),
            pltpu.VMEM((tc, ac, nk), f32),
            pltpu.VMEM((7, tc, ac, nk), f32),
            pltpu.VMEM((2, 2, 5, tc, nk), f32),
            pltpu.VMEM((2, 2, 5, tc, nk), f32),
            pltpu.VMEM((lon, tiles1, 8, nk), f32),
            pltpu.VMEM((lon, tiles2, 8, nk), f32),
            pltpu.VMEM((lon, tiles1, 8, nk), f32),
            pltpu.VMEM((lon, tiles2, 8, nk), f32),
            pltpu.SemaphoreType.DMA((4,)),
            pltpu.SemaphoreType.DMA((2, 2)),
            pltpu.SemaphoreType.DMA((2, 2)),
            pltpu.SemaphoreType.DMA((2, 2)),
            pltpu.SemaphoreType.DMA((2, 2)),
            pltpu.SemaphoreType.DMA((2, lon)),
            pltpu.SemaphoreType.DMA((2, lon)),
        ],
        compiler_params=pltpu.CompilerParams(
            collective_id=0, has_side_effects=True, vmem_limit_bytes=48 * 1024 * 1024
        ),
    )(
        jnp.asarray(polar_constants(tc, ac, lon, colat)),
        jnp.asarray(row_constants(tc, ac, lon, colat)),
        portion,
        slot,
        weights,
        angle,
        flow,
        pres,
        visc,
        heat,
    )


def solution(mesh):
    return jax.shard_map(
        functools.partial(body, mesh.shape["lon"], mesh.shape["colat"]),
        mesh=mesh,
        in_specs=(
            P("panel", None, "colat", "lon", None),
            P("panel", "colat", "lon", None),
            P("panel", "colat", "lon", None),
            P("panel", "colat", "lon", None),
            P("panel", None),
            P("panel", None),
            P("panel", None, None),
            P("panel", None),
        ),
        out_specs=(P("panel", None, "colat", "lon", None), P("panel", "colat", "lon", None)),
        check_vma=False,
    )
```

time: 93 us -> 31.3 us (0.34)
  starting transfers between devices: 32.9 us -> 0 us
  waiting for transfers between devices: 23.8 us -> 0 us
  Pallas kernels: 0 us -> 21.2 us
  other arithmetic: 14.9 us -> 0 us
  local copies, waits for them, and re-layouts: 19.3 us -> 9.07 us
    all_to_all x3 -> x0, waiting for transfers between devices: 21.2 us -> none  [the longest x2 14.9 us: body(): lax.all_to_all(moved_vals, 'lon', split_axis=0, concat_axis=0, tiled=True)]
    pallas_call x0 -> x1, Pallas kernels: none -> 21.2 us  [body(): pl.pallas_call(functools.partial(kernel, (tc, ac, nk, lon, colat, slots,...]
    ppermute x11 -> x0, starting transfers between devices: 18.1 us -> none  [the longest x4 7.81 us: extended(): lax.ppermute(tail, axis, [(i, (i + 1) % count) for i in range(ends)])]
    all_to_all x3 -> x0, starting transfers between devices: 14.8 us -> none  [the longest x2 7.81 us: body(): lax.all_to_all(moved_vals, 'lon', split_axis=0, concat_axis=0, tiled=True)]
    gather x12 -> x0, local copies, waits for them, and re-layouts: 7.63 us -> none  [the longest x2 1.19 us: body(): corner_last = flattened[:, donor_cells + azimuth_cells + 1]]
    unnamed x18 -> x22, local copies, waits for them, and re-layouts: 1.72 us -> 9.07 us
    scatter-add x6 -> x0, other arithmetic: 4.53 us -> none  [the longest x2 3.27 us: body(): ghosts = empty.at[jnp.where(west_side, routed_ids % polar_cells, jnp.wher...]
    scatter x1 -> x0, local copies, waits for them, and re-layouts: 2.91 us -> none  [body(): jnp.full((slot_total,), -1, jnp.int32).at[slot_place]]
  transfers between devices with their start and end apart: 14 -> 0, of which waited for: 4 -> 0; matrix products, arithmetic and copies ran while one was open for 13% -> 0% of each run, Pallas kernels for 0% -> 0%
where the time goes in v1:
time: 31.3 us; the launch traced here: 31 us
  Pallas kernels  21.2 us (68%)
  local copies, waits for them, and re-layouts  9.07 us (29%)
  between operations  0.66 us (2%)
    pallas_call x1, Pallas kernels, body(): pl.pallas_call(functools.partial(kernel, (tc, ac, nk, lon, colat, slots,...  21.2 us
    unnamed x22, local copies, waits for them, and re-layouts  9.07 us

profile of v1, /device:TPU:0, one launch (start us, length us, event | category | flops | bytes accessed | tf_op | source)
XLA Modules:
  0.0 31.0 jit_solution(17064232430870515292)
XLA Ops:
  0.6 0.0 copy-start
  0.6 1.0 %copy-done = f32[1,3,8,24,128]{4,3,2,1,0:T(8,128)S(1)} copy-done((f32[1,3,8,24,128]{4,3,2,1,0:T(8,128)S(1)}, f32[1,3,8,24,128]{4,3,2,1,0:T(8,128)}, u32[]{:S(2)}) %copy-start) | copy-done | bytes 294936
  1.6 0.0 copy-start.1
  1.6 0.9 %copy-done.1 = f32[1,8,24,128]{3,2,1,0:T(8,128)S(1)} copy-done((f32[1,8,24,128]{3,2,1,0:T(8,128)S(1)}, f32[1,8,24,128]{3,2,1,0:T(8,128)}, u32[]{:S(2)}) %copy-start.1) | copy-done | bytes 98328
  2.5 0.0 copy-start.2
  2.5 0.9 %copy-done.2 = f32[1,8,24,128]{3,2,1,0:T(8,128)S(1)} copy-done((f32[1,8,24,128]{3,2,1,0:T(8,128)S(1)}, f32[1,8,24,128]{3,2,1,0:T(8,128)}, u32[]{:S(2)}) %copy-start.2) | copy-done | bytes 98328
  3.4 0.0 copy-start.3
  3.4 0.9 %copy-done.3 = f32[1,8,24,128]{3,2,1,0:T(8,128)S(1)} copy-done((f32[1,8,24,128]{3,2,1,0:T(8,128)S(1)}, f32[1,8,24,128]{3,2,1,0:T(8,128)}, u32[]{:S(2)}) %copy-start.3) | copy-done | bytes 98328
  4.3 0.0 copy-start.4
  4.3 0.7 %copy-done.4 = s32[3,416]{1,0:T(4,128)S(1)} copy-done((s32[3,416]{1,0:T(4,128)S(1)}, s32[3,416]{1,0:T(4,128)}, u32[]{:S(2)}) %copy-start.4) | copy-done | bytes 5016
  5.0 0.0 copy-start.5
  5.0 0.7 %copy-done.5 = f32[1,2,416]{2,1,0:T(2,128)S(1)} copy-done((f32[1,2,416]{2,1,0:T(2,128)S(1)}, f32[1,2,416]{2,1,0:T(2,128)}, u32[]{:S(2)}) %copy-start.5) | copy-done | bytes 3352
  5.7 0.0 copy-start.6
  5.7 0.7 %copy-done.6 = s32[1,416]{1,0:T(1,128)S(1)} copy-done((s32[1,416]{1,0:T(1,128)S(1)}, s32[1,416]{1,0:T(1,128)}, u32[]{:S(2)}) %copy-start.6) | copy-done | bytes 1688
  6.3 0.0 copy-start.7
  6.3 0.7 %copy-done.7 = s32[1,416]{1,0:T(1,128)S(1)} copy-done((s32[1,416]{1,0:T(1,128)S(1)}, s32[1,416]{1,0:T(1,128)}, u32[]{:S(2)}) %copy-start.7) | copy-done | bytes 1688
  7.0 0.0 copy-start.8
  7.0 0.7 %copy-done.8 = f32[1,416]{1,0:T(1,128)S(1)} copy-done((f32[1,416]{1,0:T(1,128)S(1)}, f32[1,416]{1,0:T(1,128)}, u32[]{:S(2)}) %copy-start.8) | copy-done | bytes 1688
  7.7 0.0 copy-start.9
  7.7 0.7 %copy-done.9 = f32[128]{0:T(128)S(1)} copy-done((f32[128]{0:T(128)S(1)}, f32[128]{0:T(128)}, u32[]{:S(2)}) %copy-start.9) | copy-done | bytes 536
  8.4 21.2 %shard_map.113 = (f32[1,3,8,24,128]{4,3,2,1,0:T(8,128)S(1)}, f32[1,8,24,128]{3,2,1,0:T(8,128)S(1)}) custom-call(f32[128]{0:T(128)S(1)} %copy-done.9, s32[3,416]{1,0:T(4,128)S(1)} %copy-done.4, s32[1,416]{1,0:T(1,128)S(1)} %copy-done.6, s32[1,416]{1,0:T(1,128)S(1)} %copy-done.7, f32[1,2,416]{2,1,0:T(2,128)S(1)} %copy-done.5, f32[1,416]{1,0:T(1,128)S(1)} %copy-done.8, ...), custom_call_target="tpu_custom_call" | custom-call | tf_op jit(solution)/shard_map/pallas_call | solution.py:427
  29.6 0.7 %copy.14 = f32[1,3,8,24,128]{4,3,2,1,0:T(8,128)} copy(f32[1,3,8,24,128]{4,3,2,1,0:T(8,128)S(1)} %get-tuple-element.4) | data formatting | bytes 589824
  30.3 0.6 %copy.15 = f32[1,8,24,128]{3,2,1,0:T(8,128)} copy(f32[1,8,24,128]{3,2,1,0:T(8,128)S(1)} %get-tuple-element.5) | data formatting | bytes 196608
Async XLA Ops:
  0.6 1.0 %copy-start = (f32[1,3,8,24,128]{4,3,2,1,0:T(8,128)S(1)}, f32[1,3,8,24,128]{4,3,2,1,0:T(8,128)}, u32[]{:S(2)}) copy-start(f32[1,3,8,24,128]{4,3,2,1,0:T(8,128)} %flow_hbm.1) | copy-start | bytes 884740
  1.6 0.9 %copy-start.1 = (f32[1,8,24,128]{3,2,1,0:T(8,128)S(1)}, f32[1,8,24,128]{3,2,1,0:T(8,128)}, u32[]{:S(2)}) copy-start(f32[1,8,24,128]{3,2,1,0:T(8,128)} %pres_hbm.1) | copy-start | bytes 294916
  2.5 0.9 %copy-start.2 = (f32[1,8,24,128]{3,2,1,0:T(8,128)S(1)}, f32[1,8,24,128]{3,2,1,0:T(8,128)}, u32[]{:S(2)}) copy-start(f32[1,8,24,128]{3,2,1,0:T(8,128)} %visc_hbm.1) | copy-start | bytes 294916
  3.4 0.9 %copy-start.3 = (f32[1,8,24,128]{3,2,1,0:T(8,128)S(1)}, f32[1,8,24,128]{3,2,1,0:T(8,128)}, u32[]{:S(2)}) copy-start(f32[1,8,24,128]{3,2,1,0:T(8,128)} %heat_hbm.1) | copy-start | bytes 294916
  4.3 0.7 %copy-start.4 = (s32[3,416]{1,0:T(4,128)S(1)}, s32[3,416]{1,0:T(4,128)}, u32[]{:S(2)}) copy-start(s32[3,416]{1,0:T(4,128)} %constant.5.clone.const_ref) | copy-start | bytes 14980
  5.0 0.7 %copy-start.5 = (f32[1,2,416]{2,1,0:T(2,128)S(1)}, f32[1,2,416]{2,1,0:T(2,128)}, u32[]{:S(2)}) copy-start(f32[1,2,416]{2,1,0:T(2,128)} %weight_ref.1) | copy-start | bytes 9988
  5.7 0.7 %copy-start.6 = (s32[1,416]{1,0:T(1,128)S(1)}, s32[1,416]{1,0:T(1,128)}, u32[]{:S(2)}) copy-start(s32[1,416]{1,0:T(1,128)} %portion_ref.1) | copy-start | bytes 4996
  6.3 0.7 %copy-start.7 = (s32[1,416]{1,0:T(1,128)S(1)}, s32[1,416]{1,0:T(1,128)}, u32[]{:S(2)}) copy-start(s32[1,416]{1,0:T(1,128)} %slot_ref.1) | copy-start | bytes 4996
  7.0 0.7 %copy-start.8 = (f32[1,416]{1,0:T(1,128)S(1)}, f32[1,416]{1,0:T(1,128)}, u32[]{:S(2)}) copy-start(f32[1,416]{1,0:T(1,128)} %angle_ref.1) | copy-start | bytes 4996
  7.7 0.7 %copy-start.9 = (f32[128]{0:T(128)S(1)}, f32[128]{0:T(128)}, u32[]{:S(2)}) copy-start(f32[128]{0:T(128)} %constant.4.clone.polar_ref) | copy-start | bytes 1540

commit v2 on v1

--- a/solution.py
+++ b/solution.py
@@ -44,24 +44,120 @@
     return table.reshape(-1).astype(np.float32)
 
 
+def above(x):
+    return pltpu.roll(x, x.shape[1] - 1, 1)
+
+
+def below(x):
+    return pltpu.roll(x, 1, 1)
+
+
+def radial(nk):
+    lane = lax.broadcasted_iota(jnp.int32, (1, nk), 1)
+    radius = INNER_RATIO * nk + lane.astype(jnp.float32) + 0.5
+    inv = 1.0 / radius
+    top, bottom = lane == nk - 1, lane == 0
+    return {
+        "inv": inv,
+        "top": top,
+        "bottom": bottom,
+        "up_geo": 0.5 * ((radius + 0.5) * inv) ** 2,
+        "down_geo": 0.5 * ((radius - 0.5) * inv) ** 2,
+        "grad_up": jnp.where(top, 0.0, 0.5),
+        "grad_down": jnp.where(bottom, 0.0, 0.5),
+        "div_up": jnp.where(top, 0.0, 0.5 * ((radius + 1.0) * inv) ** 2),
+        "div_down": jnp.where(bottom, 0.0, 0.5 * ((radius - 1.0) * inv) ** 2),
+    }
+
+
+def smoothed(pad, t, ac, lane, factors, steps):
+    b_up, b_dn, b_n, b_s, b_w, b_e, d, e, heat = factors
+    polar, azimuth, div_n, div_s = steps
+    inner = pl.ds(LEFT, ac)
+
+    def near(f):
+        return (
+            pad[f, t + 1, inner, :],
+            pad[f, t, inner, :],
+            pad[f, t + 2, inner, :],
+            pad[f, t + 1, pl.ds(LEFT - 1, ac), :],
+            pad[f, t + 1, pl.ds(LEFT + 1, ac), :],
+        )
+
+    pc, pn, ps, pw, pe = near(3)
+    forcing = (
+        heat - d * (lane["grad_up"] * above(pc) - lane["grad_down"] * below(pc)),
+        d * ((pn - ps) * polar),
+        d * ((pw - pe) * azimuth),
+    )
+    new, div = [], None
+    for f in range(3):
+        w, wn, ws, ww, we = near(f)
+        wu, wd = above(w), below(w)
+        total = b_up * wu + b_dn * wd + b_n * wn + b_s * ws + b_w * ww + b_e * we
+        new.append((1.0 - OMEGA_VELOCITY) * w + (total + forcing[f]))
+        if f == 0:
+            div = lane["div_up"] * wu - lane["div_down"] * wd
+        elif f == 1:
+            div = div + (div_s * ws - div_n * wn)
+        else:
+            div = div + (we - ww) * azimuth
+    new.append(pc - e * div)
+    return new
+
+
+def last_kernel(dims, pad, coef, geo, vel_hbm, pres_hbm, vel, pres, sem):
+    tc, ac, nk = dims
+    lane = radial(nk)
+    parts = 2 if tc % 2 == 0 else 1
+    size = tc // parts
+
+    def row(t, carry):
+        factors = [coef[i, t] for i in range(9)]
+        steps = [geo[i, t, 0:1, :] for i in range(4)]
+        new = smoothed(pad, t, ac, lane, factors, steps)
+        for f in range(3):
+            vel[f, t] = new[f]
+        pres[t] = new[3]
+        return carry
+
+    copies = []
+    for part in range(parts):
+        lo, hi = part * size, (part + 1) * size
+        lax.fori_loop(lo, hi, row, 0)
+        copies += [
+            pltpu.make_async_copy(vel.at[:, lo:hi], vel_hbm.at[0, :, lo:hi], sem.at[part, 0]),
+            pltpu.make_async_copy(pres.at[lo:hi], pres_hbm.at[0, lo:hi], sem.at[part, 1]),
+        ]
+        for copy in copies[-2:]:
+            copy.start()
+    for copy in copies:
+        copy.wait()
+
+
 def kernel(
     dims,
+    polar_hbm,
+    const_hbm,
+    portion_hbm,
+    slot_hbm,
+    weight_hbm,
+    angle_hbm,
+    flow_hbm,
+    pres_hbm,
+    visc_hbm,
+    heat_hbm,
+    pad2,
+    coef,
+    geo,
+    pad1,
+    heat,
     polar_ref,
     const_ref,
     portion_ref,
     slot_ref,
     weight_ref,
     angle_ref,
-    flow_hbm,
-    pres_hbm,
-    visc_hbm,
-    heat_hbm,
-    vel_out,
-    pres_out,
-    pad1,
-    pad2,
-    heat,
-    coef,
     lon_send,
     lon_recv,
     send1,
@@ -93,8 +189,16 @@
         pltpu.make_async_copy(pres_hbm.at[0], pad1.at[3, 1 : tc + 1, inner, :], in_sem.at[1]),
         pltpu.make_async_copy(visc_hbm.at[0], pad1.at[4, 1 : tc + 1, inner, :], in_sem.at[2]),
         pltpu.make_async_copy(heat_hbm.at[0], heat, in_sem.at[3]),
+        pltpu.make_async_copy(polar_hbm, polar_ref, in_sem.at[4]),
     ]
-    for copy in local:
+    tables = [
+        pltpu.make_async_copy(const_hbm, const_ref, in_sem.at[5]),
+        pltpu.make_async_copy(portion_hbm, portion_ref, in_sem.at[6]),
+        pltpu.make_async_copy(slot_hbm, slot_ref, in_sem.at[7]),
+        pltpu.make_async_copy(weight_hbm, weight_ref, in_sem.at[8]),
+        pltpu.make_async_copy(angle_hbm, angle_ref, in_sem.at[9]),
+    ]
+    for copy in tables + local:
         copy.start()
 
     barrier = pltpu.get_barrier_semaphore()
@@ -114,6 +218,9 @@
     pl.when(has["e"])(lambda: greet(lon=l + 1))
     pl.when(has["n"])(lambda: greet(colat=c - 1))
     pl.when(has["s"])(lambda: greet(colat=c + 1))
+
+    for copy in tables:
+        copy.wait()
 
     target = const_ref[0:1, :]
     serving = (portion_ref[...] == l) & (const_ref[1:2, :] == c)
@@ -302,90 +409,40 @@
                 def _():
                     pad[f, tc + 1, inner, :] = band
 
-    lane = lax.broadcasted_iota(jnp.int32, (1, nk), 1)
-    radius = INNER_RATIO * nk + lane.astype(jnp.float32) + 0.5
-    inv = 1.0 / radius
-    inv2 = inv * inv
-    top, bottom = lane == nk - 1, lane == 0
-    up_geo = 0.5 * ((radius + 0.5) * inv) ** 2
-    down_geo = 0.5 * ((radius - 0.5) * inv) ** 2
-    grad_up = jnp.where(top, 0.0, 0.5)
-    grad_down = jnp.where(bottom, 0.0, 0.5)
-    div_up = jnp.where(top, 0.0, 0.5 * ((radius + 1.0) * inv) ** 2)
-    div_down = jnp.where(bottom, 0.0, 0.5 * ((radius - 1.0) * inv) ** 2)
-
-    def above(x):
-        return pltpu.roll(x, nk - 1, 1)
-
-    def below(x):
-        return pltpu.roll(x, 1, 1)
-
-    def smooth(sweep):
-        pad = pads[sweep]
-
-        def row(t, carry):
-            scalar = lambda i: polar_ref[(c * tc + t) * SCALARS + i]
-
-            def near(f):
-                return (
-                    pad[f, t + 1, inner, :],
-                    pad[f, t, inner, :],
-                    pad[f, t + 2, inner, :],
-                    pad[f, t + 1, pl.ds(LEFT - 1, ac), :],
-                    pad[f, t + 1, pl.ds(LEFT + 1, ac), :],
-                )
-
-            if sweep == 0:
-                e, en, es, ew, ee = near(4)
-                e_up = jnp.where(top, e, above(e))
-                e_dn = jnp.where(bottom, e, below(e))
-                a_up = (e + e_up) * up_geo
-                a_dn = (e + e_dn) * down_geo
-                a_n = (e + en) * (scalar(0) * inv2)
-                a_s = (e + es) * (scalar(1) * inv2)
-                h2 = scalar(2) * inv2
-                a_w = (e + ew) * h2
-                a_e = (e + ee) * h2
-                d = OMEGA_VELOCITY / (a_up + a_dn + a_n + a_s + a_w + a_e)
-                b_up = jnp.where(top, 0.0, a_up * d)
-                b_dn = jnp.where(bottom, 0.0, a_dn * d)
-                b_n, b_s, b_w, b_e = a_n * d, a_s * d, a_w * d, a_e * d
-                for i, b in enumerate((b_up, b_dn, b_n, b_s, b_w, b_e, d)):
-                    coef[i, t] = b
-            else:
-                b_up, b_dn, b_n, b_s, b_w, b_e, d = [coef[i, t] for i in range(7)]
-                e = pad1[4, t + 1, inner, :]
-            pc, pn, ps, pw, pe = near(3)
-            az = scalar(4) * inv
-            forcing = (
-                heat[t] - (grad_up * above(pc) - grad_down * below(pc)),
-                (pn - ps) * (scalar(3) * inv),
-                (pw - pe) * az,
-            )
-            new = []
-            div = None
-            for f in range(3):
-                w, wn, ws, ww, we = near(f)
-                wu, wd = above(w), below(w)
-                total = b_up * wu + b_dn * wd + b_n * wn + b_s * ws + b_w * ww + b_e * we
-                new.append((1.0 - OMEGA_VELOCITY) * w + (total + d * forcing[f]))
-                if f == 0:
-                    div = div_up * wu - div_down * wd
-                elif f == 1:
-                    div = div + (scalar(6) * ws - scalar(5) * wn) * inv
-                else:
-                    div = div + (we - ww) * az
-            new.append(pc - OMEGA_PRESSURE * e * div)
-            if sweep == 0:
-                for f in range(4):
-                    pad2[f, t + 1, inner, :] = new[f]
-            else:
-                for f in range(3):
-                    vel_out[0, f, t] = new[f]
-                pres_out[0, t] = new[3]
-            return carry
-
-        lax.fori_loop(0, tc, row, 0)
+    lane = radial(nk)
+    top, bottom, inv = lane["top"], lane["bottom"], lane["inv"]
+
+    def first(t, carry):
+        scalar = lambda i: polar_ref[(c * tc + t) * SCALARS + i]
+        inv2 = inv * inv
+        e = pad1[4, t + 1, inner, :]
+        a_up = (e + jnp.where(top, e, above(e))) * lane["up_geo"]
+        a_dn = (e + jnp.where(bottom, e, below(e))) * lane["down_geo"]
+        a_n = (e + pad1[4, t, inner, :]) * (scalar(0) * inv2)
+        a_s = (e + pad1[4, t + 2, inner, :]) * (scalar(1) * inv2)
+        h2 = scalar(2) * inv2
+        a_w = (e + pad1[4, t + 1, pl.ds(LEFT - 1, ac), :]) * h2
+        a_e = (e + pad1[4, t + 1, pl.ds(LEFT + 1, ac), :]) * h2
+        d = OMEGA_VELOCITY / (a_up + a_dn + a_n + a_s + a_w + a_e)
+        factors = [
+            jnp.where(top, 0.0, a_up * d),
+            jnp.where(bottom, 0.0, a_dn * d),
+            a_n * d,
+            a_s * d,
+            a_w * d,
+            a_e * d,
+            d,
+            OMEGA_PRESSURE * e,
+            heat[t] * d,
+        ]
+        steps = [scalar(i) * inv for i in (3, 4, 5, 6)]
+        for i, factor in enumerate(factors):
+            coef[i, t] = factor
+        for i, step in enumerate(steps):
+            geo[i, t] = jnp.broadcast_to(step, (8, nk))
+        for f, value in enumerate(smoothed(pad1, t, ac, lane, factors, steps)):
+            pad2[f, t + 1, inner, :] = value
+        return carry
 
     greeted = lon + sum(has[side].astype(jnp.int32) for side in "wens")
     for copy in local:
@@ -398,14 +455,13 @@
     wait_all(0)
     where_to = placing()
     assemble(0, where_to)
-    smooth(0)
+    lax.fori_loop(0, tc, first, 0)
     stage_lon(1)
     start_halos(1)
     gather(1)
     start_panel(1)
     wait_all(1)
     assemble(1, where_to)
-    smooth(1)
     wait_sent(0)
     wait_sent(1)
 
@@ -419,28 +475,37 @@
         slots *= 2
     pack = 8 // slots
     tiles1, tiles2 = -(-6 // pack), -(-4 // pack)
-    f32 = jnp.float32
+    f32, i32 = jnp.float32, jnp.int32
     vmem = pl.BlockSpec(memory_space=pltpu.VMEM)
-    hbm = pl.BlockSpec(memory_space=pl.ANY)
-    smem = pl.BlockSpec(memory_space=pltpu.SMEM)
+    hbm = pl.BlockSpec(memory_space=pltpu.HBM)
     wide = LEFT + ac + 8
-    return pl.pallas_call(
+    polar = jnp.asarray(polar_constants(tc, ac, lon, colat))
+    constants = jnp.asarray(row_constants(tc, ac, lon, colat))
+    pad, coef, geo = pl.pallas_call(
         functools.partial(kernel, (tc, ac, nk, lon, colat, slots, pack)),
-        out_shape=(jax.ShapeDtypeStruct(flow.shape, f32), jax.ShapeDtypeStruct(pres.shape, f32)),
-        in_specs=[smem] + [vmem] * 5 + [hbm] * 4,
-        out_specs=(vmem, vmem),
+        out_shape=(
+            jax.ShapeDtypeStruct((4, tc + 2, wide, nk), f32),
+            jax.ShapeDtypeStruct((9, tc, ac, nk), f32),
+            jax.ShapeDtypeStruct((4, tc, 8, nk), f32),
+        ),
+        in_specs=[hbm] * 10,
+        out_specs=(vmem, vmem, vmem),
         scratch_shapes=[
             pltpu.VMEM((5, tc + 2, wide, nk), f32),
-            pltpu.VMEM((4, tc + 2, wide, nk), f32),
             pltpu.VMEM((tc, ac, nk), f32),
-            pltpu.VMEM((7, tc, ac, nk), f32),
+            pltpu.SMEM(polar.shape, f32),
+            pltpu.VMEM(constants.shape, i32),
+            pltpu.VMEM(portion.shape, i32),
+            pltpu.VMEM(slot.shape, i32),
+            pltpu.VMEM(weights.shape, f32),
+            pltpu.VMEM(angle.shape, f32),
             pltpu.VMEM((2, 2, 5, tc, nk), f32),
             pltpu.VMEM((2, 2, 5, tc, nk), f32),
             pltpu.VMEM((lon, tiles1, 8, nk), f32),
             pltpu.VMEM((lon, tiles2, 8, nk), f32),
             pltpu.VMEM((lon, tiles1, 8, nk), f32),
             pltpu.VMEM((lon, tiles2, 8, nk), f32),
-            pltpu.SemaphoreType.DMA((4,)),
+            pltpu.SemaphoreType.DMA((10,)),
             pltpu.SemaphoreType.DMA((2, 2)),
             pltpu.SemaphoreType.DMA((2, 2)),
             pltpu.SemaphoreType.DMA((2, 2)),
@@ -449,20 +514,21 @@
             pltpu.SemaphoreType.DMA((2, lon)),
         ],
         compiler_params=pltpu.CompilerParams(
-            collective_id=0, has_side_effects=True, vmem_limit_bytes=48 * 1024 * 1024
+            collective_id=0, has_side_effects=True, vmem_limit_bytes=32 * 1024 * 1024
         ),
-    )(
-        jnp.asarray(polar_constants(tc, ac, lon, colat)),
-        jnp.asarray(row_constants(tc, ac, lon, colat)),
-        portion,
-        slot,
-        weights,
-        angle,
-        flow,
-        pres,
-        visc,
-        heat,
-    )
+    )(*(pltpu.with_memory_space_constraint(x, pltpu.HBM) for x in (polar, constants, portion, slot, weights, angle, flow, pres, visc, heat)))
+    return pl.pallas_call(
+        functools.partial(last_kernel, (tc, ac, nk)),
+        out_shape=(jax.ShapeDtypeStruct(flow.shape, f32), jax.ShapeDtypeStruct(pres.shape, f32)),
+        in_specs=[vmem] * 3,
+        out_specs=(hbm, hbm),
+        scratch_shapes=[
+            pltpu.VMEM(flow.shape[1:], f32),
+            pltpu.VMEM(pres.shape[1:], f32),
+            pltpu.SemaphoreType.DMA((2, 2)),
+        ],
+        compiler_params=pltpu.CompilerParams(vmem_limit_bytes=32 * 1024 * 1024),
+    )(pad, coef, geo)
 
 
 def solution(mesh):

time: 31.3 us -> 22.2 us (0.71)
  local copies, waits for them, and re-layouts: 9.07 us -> 0 us
    unnamed x22 -> x0, local copies, waits for them, and re-layouts: 9.07 us -> none
    pallas_call x0 -> x1, Pallas kernels: none -> 1.53 us  [body(): pl.pallas_call(functools.partial(last_kernel, (tc, ac, nk)), out_shape=(j...]
    pallas_call x1, Pallas kernels: 21.2 us -> 19.8 us  [body(): pl.pallas_call(functools.partial(kernel, (tc, ac, nk, lon, colat, slots,...]
where the time goes in v2:
time: 22.2 us; the launch traced here: 22 us
  Pallas kernels  21.3 us (96%)
  between operations  0.64 us (3%)
    pallas_call x1, Pallas kernels, body(): pl.pallas_call(functools.partial(kernel, (tc, ac, nk, lon, colat, slots,...  19.8 us
    pallas_call x1, Pallas kernels, body(): pl.pallas_call(functools.partial(last_kernel, (tc, ac, nk)), out_shape=(j...  1.53 us

profile of v2, /device:TPU:0, one launch (start us, length us, event | category | flops | bytes accessed | tf_op | source)
XLA Modules:
  0.0 22.0 jit_solution(13862041996814142403)
XLA Ops:
  0.6 19.8 %shard_map.113 = (f32[4,10,40,128]{3,2,1,0:T(8,128)S(1)}, f32[9,8,24,128]{3,2,1,0:T(8,128)S(1)}, f32[4,8,8,128]{3,2,1,0:T(8,128)S(1)}) custom-call(f32[128]{0:T(128)} %constant.4.clone.polar_hbm, s32[3,416]{1,0:T(4,128)} %constant.5.clone.const_hbm, s32[1,416]{1,0:T(1,128)} %portion_hbm.1, s32[1,416]{1,0:T(1,128)} %slot_hbm.1, f32[1,2,416]{2,1,0:T(2,128)} %weight_hbm.1, ...), custom_call_target="tpu_custom_call" | custom-call | tf_op jit(solution)/shard_map/pallas_call | solution.py:484
  20.4 1.5 %shard_map.114 = (f32[1,3,8,24,128]{4,3,2,1,0:T(8,128)}, f32[1,8,24,128]{3,2,1,0:T(8,128)}) custom-call(f32[4,10,40,128]{3,2,1,0:T(8,128)S(1)} %get-tuple-element.5.pad, f32[9,8,24,128]{3,2,1,0:T(8,128)S(1)} %get-tuple-element.6.coef, f32[4,8,8,128]{3,2,1,0:T(8,128)S(1)} %get-tuple-element.7.geo), custom_call_target="tpu_custom_call" | custom-call | tf_op jit(solution)/shard_map/pallas_call | solution.py:520

commit v3 on v2

--- a/solution.py
+++ b/solution.py
@@ -45,15 +45,23 @@
 
 
 def above(x):
-    return pltpu.roll(x, x.shape[1] - 1, 1)
+    return pltpu.roll(x, x.shape[2] - 1, 2)
 
 
 def below(x):
-    return pltpu.roll(x, 1, 1)
+    return pltpu.roll(x, 1, 2)
+
+
+def west(j, nj):
+    return pl.ds(LEFT + j - 1, nj)
+
+
+def east(j, nj):
+    return pl.ds(LEFT + j + 1, nj)
 
 
 def radial(nk):
-    lane = lax.broadcasted_iota(jnp.int32, (1, nk), 1)
+    lane = lax.broadcasted_iota(jnp.int32, (1, 1, nk), 2)
     radius = INNER_RATIO * nk + lane.astype(jnp.float32) + 0.5
     inv = 1.0 / radius
     top, bottom = lane == nk - 1, lane == 0
@@ -70,18 +78,18 @@
     }
 
 
-def smoothed(pad, t, ac, lane, factors, steps):
+def smoothed(pad, t, nt, j, nj, lane, factors, steps):
     b_up, b_dn, b_n, b_s, b_w, b_e, d, e, heat = factors
     polar, azimuth, div_n, div_s = steps
-    inner = pl.ds(LEFT, ac)
+    here, cols = pl.ds(t + 1, nt), pl.ds(LEFT + j, nj)
 
     def near(f):
         return (
-            pad[f, t + 1, inner, :],
-            pad[f, t, inner, :],
-            pad[f, t + 2, inner, :],
-            pad[f, t + 1, pl.ds(LEFT - 1, ac), :],
-            pad[f, t + 1, pl.ds(LEFT + 1, ac), :],
+            pad[f, here, cols, :],
+            pad[f, pl.ds(t, nt), cols, :],
+            pad[f, pl.ds(t + 2, nt), cols, :],
+            pad[f, here, west(j, nj), :],
+            pad[f, here, east(j, nj), :],
         )
 
     pc, pn, ps, pw, pe = near(3)
@@ -106,31 +114,11 @@
     return new
 
 
-def last_kernel(dims, pad, coef, geo, vel_hbm, pres_hbm, vel, pres, sem):
-    tc, ac, nk = dims
-    lane = radial(nk)
-    parts = 2 if tc % 2 == 0 else 1
-    size = tc // parts
-
-    def row(t, carry):
-        factors = [coef[i, t] for i in range(9)]
-        steps = [geo[i, t, 0:1, :] for i in range(4)]
-        new = smoothed(pad, t, ac, lane, factors, steps)
-        for f in range(3):
-            vel[f, t] = new[f]
-        pres[t] = new[3]
-        return carry
-
-    copies = []
-    for part in range(parts):
-        lo, hi = part * size, (part + 1) * size
-        lax.fori_loop(lo, hi, row, 0)
-        copies += [
-            pltpu.make_async_copy(vel.at[:, lo:hi], vel_hbm.at[0, :, lo:hi], sem.at[part, 0]),
-            pltpu.make_async_copy(pres.at[lo:hi], pres_hbm.at[0, lo:hi], sem.at[part, 1]),
-        ]
-        for copy in copies[-2:]:
-            copy.start()
+def copy_out(vel, pres, vel_hbm, pres_hbm, sem):
+    copies = [pltpu.make_async_copy(vel.at[f], vel_hbm.at[0, f], sem.at[f]) for f in range(3)]
+    copies.append(pltpu.make_async_copy(pres, pres_hbm.at[0], sem.at[3]))
+    for copy in copies:
+        copy.start()
     for copy in copies:
         copy.wait()
 
@@ -147,6 +135,8 @@
     pres_hbm,
     visc_hbm,
     heat_hbm,
+    vel,
+    pres,
     pad2,
     coef,
     geo,
@@ -198,10 +188,11 @@
         pltpu.make_async_copy(weight_hbm, weight_ref, in_sem.at[8]),
         pltpu.make_async_copy(angle_hbm, angle_ref, in_sem.at[9]),
     ]
-    for copy in tables + local:
-        copy.start()
 
     barrier = pltpu.get_barrier_semaphore()
+
+    def distant(k):
+        return l ^ (lon - 1 - k) if lon & (lon - 1) == 0 else lax.rem(l + k, lon)
 
     def greet(**where):
         pl.semaphore_signal(
@@ -209,7 +200,7 @@
         )
 
     def greet_panel(k, carry):
-        greet(panel=other, lon=lax.rem(l + k, lon))
+        greet(panel=other, lon=distant(k))
         return carry
 
     lax.fori_loop(0, lon, greet_panel, 0)
@@ -219,6 +210,8 @@
     pl.when(has["n"])(lambda: greet(colat=c - 1))
     pl.when(has["s"])(lambda: greet(colat=c + 1))
 
+    for copy in tables + local:
+        copy.start()
     for copy in tables:
         copy.wait()
 
@@ -336,17 +329,18 @@
 
     def start_panel(sweep):
         def one(k, carry):
-            panel_copy(sweep, lax.rem(l + k, lon), l).start()
+            panel_copy(sweep, distant(k), l).start()
             return carry
 
         lax.fori_loop(0, lon, one, 0)
 
-    def wait_all(sweep):
+    def wait_halos(sweep):
         pl.when(has["e"])(lambda: lon_copy(sweep, 0).wait_recv())
         pl.when(has["w"])(lambda: lon_copy(sweep, 1).wait_recv())
         pl.when(has["s"])(lambda: colat_copy(sweep, 0).wait_recv())
         pl.when(has["n"])(lambda: colat_copy(sweep, 1).wait_recv())
 
+    def wait_panel(sweep):
         def one(k, carry):
             panel_copy(sweep, k, k).wait_recv()
             return carry
@@ -378,51 +372,87 @@
             place = lax.broadcasted_iota(jnp.int32, (packed, ghosts), 1).astype(jnp.float32) + 1.0
             hit = (total[:, :ghosts] == place) & (block_of[:, :ghosts] == h)
             blocks.append(jnp.where(hit, 1.0, 0.0))
-        return jnp.concatenate(blocks, axis=1)
+        return jnp.concatenate(blocks, axis=1).astype(jnp.bfloat16)
+
+    def place_halos(sweep):
+        pad = pads[sweep]
+
+        @pl.when(has["w"])
+        def _():
+            for f in range(counts[sweep]):
+                pad[f, 1 : tc + 1, LEFT - 1, :] = lon_recv[sweep, 1, f]
+
+        @pl.when(has["e"])
+        def _():
+            for f in range(counts[sweep]):
+                pad[f, 1 : tc + 1, LEFT + ac, :] = lon_recv[sweep, 0, f]
 
     def assemble(sweep, where_to):
         pad, recv, n = pads[sweep], recvs[sweep], counts[sweep]
+        sides, bands = [], []
         for m in range(recv.shape[1]):
             if m * pack >= n:
                 continue
-            placed = lax.dot_general(
-                where_to,
-                recv[:, m].reshape(packed, nk),
-                (((0,), (0,)), ((), ())),
-                precision=HIGHEST,
-                preferred_element_type=jnp.float32,
-            )
+            rest = recv[:, m].reshape(packed, nk)
+            placed = None
+            for _ in range(3):
+                part = rest.astype(jnp.bfloat16)
+                rest = rest - part.astype(jnp.float32)
+                term = lax.dot_general(
+                    where_to,
+                    part,
+                    (((0,), (0,)), ((), ())),
+                    preferred_element_type=jnp.float32,
+                )
+                placed = term if placed is None else placed + term
             for h in range(pack):
-                f = m * pack + h
-                if f >= n:
-                    continue
-                mine = placed[h * ghosts : (h + 1) * ghosts]
-                side, band = mine[:tc], mine[tc:]
-                pad[f, 1 : tc + 1, LEFT - 1, :] = jnp.where(has["w"], lon_recv[sweep, 1, f], side)
-                pad[f, 1 : tc + 1, LEFT + ac, :] = jnp.where(has["e"], lon_recv[sweep, 0, f], side)
-
-                @pl.when(c == 0)
-                def _():
-                    pad[f, 0, inner, :] = band
-
-                @pl.when(c == colat - 1)
-                def _():
-                    pad[f, tc + 1, inner, :] = band
+                if m * pack + h < n:
+                    mine = placed[h * ghosts : (h + 1) * ghosts]
+                    sides.append(mine[:tc])
+                    bands.append(mine[tc:])
+
+        @pl.when(c == 0)
+        def _():
+            for f in range(n):
+                pad[f, 0, inner, :] = bands[f]
+
+        @pl.when(c == colat - 1)
+        def _():
+            for f in range(n):
+                pad[f, tc + 1, inner, :] = bands[f]
+
+        @pl.when(l == 0)
+        def _():
+            for f in range(n):
+                pad[f, 1 : tc + 1, LEFT - 1, :] = sides[f]
+
+        @pl.when(l == lon - 1)
+        def _():
+            for f in range(n):
+                pad[f, 1 : tc + 1, LEFT + ac, :] = sides[f]
 
     lane = radial(nk)
     top, bottom, inv = lane["top"], lane["bottom"], lane["inv"]
 
-    def first(t, carry):
-        scalar = lambda i: polar_ref[(c * tc + t) * SCALARS + i]
+    def first(t, nt, j, nj):
+        rows_t, cols = pl.ds(t, nt), pl.ds(j, nj)
+        scalar = lambda i: jnp.concatenate(
+            [
+                jnp.full((1, 1, nk), polar_ref[(c * tc + t + k) * SCALARS + i], jnp.float32)
+                for k in range(nt)
+            ],
+            axis=0,
+        )
         inv2 = inv * inv
-        e = pad1[4, t + 1, inner, :]
+        near = lambda dt, dj: pad1[4, pl.ds(t + 1 + dt, nt), pl.ds(LEFT + j + dj, nj), :]
+        e = near(0, 0)
         a_up = (e + jnp.where(top, e, above(e))) * lane["up_geo"]
         a_dn = (e + jnp.where(bottom, e, below(e))) * lane["down_geo"]
-        a_n = (e + pad1[4, t, inner, :]) * (scalar(0) * inv2)
-        a_s = (e + pad1[4, t + 2, inner, :]) * (scalar(1) * inv2)
+        a_n = (e + near(-1, 0)) * (scalar(0) * inv2)
+        a_s = (e + near(1, 0)) * (scalar(1) * inv2)
         h2 = scalar(2) * inv2
-        a_w = (e + pad1[4, t + 1, pl.ds(LEFT - 1, ac), :]) * h2
-        a_e = (e + pad1[4, t + 1, pl.ds(LEFT + 1, ac), :]) * h2
+        a_w = (e + pad1[4, pl.ds(t + 1, nt), west(j, nj), :]) * h2
+        a_e = (e + pad1[4, pl.ds(t + 1, nt), east(j, nj), :]) * h2
         d = OMEGA_VELOCITY / (a_up + a_dn + a_n + a_s + a_w + a_e)
         factors = [
             jnp.where(top, 0.0, a_up * d),
@@ -433,16 +463,37 @@
             a_e * d,
             d,
             OMEGA_PRESSURE * e,
-            heat[t] * d,
+            heat[rows_t, cols, :] * d,
         ]
         steps = [scalar(i) * inv for i in (3, 4, 5, 6)]
         for i, factor in enumerate(factors):
-            coef[i, t] = factor
+            coef[i, rows_t, cols, :] = factor
         for i, step in enumerate(steps):
-            geo[i, t] = jnp.broadcast_to(step, (8, nk))
-        for f, value in enumerate(smoothed(pad1, t, ac, lane, factors, steps)):
-            pad2[f, t + 1, inner, :] = value
-        return carry
+            geo[i, rows_t] = jnp.broadcast_to(step, (nt, 8, nk))
+        for f, value in enumerate(smoothed(pad1, t, nt, j, nj, lane, factors, steps)):
+            pad2[f, pl.ds(t + 1, nt), pl.ds(LEFT + j, nj), :] = value
+
+    def second(t, nt, j, nj):
+        rows_t, cols = pl.ds(t, nt), pl.ds(j, nj)
+        factors = [coef[i, rows_t, cols, :] for i in range(9)]
+        steps = [geo[i, rows_t, 0:1, :] for i in range(4)]
+        new = smoothed(pad2, t, nt, j, nj, lane, factors, steps)
+        for f in range(3):
+            vel[f, rows_t, cols, :] = new[f]
+        pres[rows_t, cols, :] = new[3]
+
+    def everywhere(update):
+        def row(t, carry):
+            update(t, 1, 0, ac)
+            return carry
+
+        lax.fori_loop(0, tc, row, 0, unroll=2)
+
+    def beside_ghosts(update):
+        pl.when(c == 0)(lambda: update(0, 1, 0, ac))
+        pl.when(c == colat - 1)(lambda: update(tc - 1, 1, 0, ac))
+        pl.when(l == 0)(lambda: update(0, tc, 0, 8))
+        pl.when(l == lon - 1)(lambda: update(0, tc, ac - 8, 8))
 
     greeted = lon + sum(has[side].astype(jnp.int32) for side in "wens")
     for copy in local:
@@ -452,16 +503,23 @@
     pl.semaphore_wait(barrier, greeted)
     start_panel(0)
     start_halos(0)
-    wait_all(0)
+    wait_halos(0)
+    place_halos(0)
+    everywhere(first)
+    wait_panel(0)
     where_to = placing()
     assemble(0, where_to)
-    lax.fori_loop(0, tc, first, 0)
+    beside_ghosts(first)
+    gather(1)
+    start_panel(1)
     stage_lon(1)
     start_halos(1)
-    gather(1)
-    start_panel(1)
-    wait_all(1)
+    wait_halos(1)
+    place_halos(1)
+    everywhere(second)
+    wait_panel(1)
     assemble(1, where_to)
+    beside_ghosts(second)
     wait_sent(0)
     wait_sent(1)
 
@@ -481,16 +539,18 @@
     wide = LEFT + ac + 8
     polar = jnp.asarray(polar_constants(tc, ac, lon, colat))
     constants = jnp.asarray(row_constants(tc, ac, lon, colat))
-    pad, coef, geo = pl.pallas_call(
+    vel_new, pres_new = pl.pallas_call(
         functools.partial(kernel, (tc, ac, nk, lon, colat, slots, pack)),
         out_shape=(
-            jax.ShapeDtypeStruct((4, tc + 2, wide, nk), f32),
-            jax.ShapeDtypeStruct((9, tc, ac, nk), f32),
-            jax.ShapeDtypeStruct((4, tc, 8, nk), f32),
+            jax.ShapeDtypeStruct(flow.shape[1:], f32),
+            jax.ShapeDtypeStruct(pres.shape[1:], f32),
         ),
         in_specs=[hbm] * 10,
-        out_specs=(vmem, vmem, vmem),
+        out_specs=(vmem, vmem),
         scratch_shapes=[
+            pltpu.VMEM((4, tc + 2, wide, nk), f32),
+            pltpu.VMEM((9, tc, ac, nk), f32),
+            pltpu.VMEM((4, tc, 8, nk), f32),
             pltpu.VMEM((5, tc + 2, wide, nk), f32),
             pltpu.VMEM((tc, ac, nk), f32),
             pltpu.SMEM(polar.shape, f32),
@@ -518,17 +578,13 @@
         ),
     )(*(pltpu.with_memory_space_constraint(x, pltpu.HBM) for x in (polar, constants, portion, slot, weights, angle, flow, pres, visc, heat)))
     return pl.pallas_call(
-        functools.partial(last_kernel, (tc, ac, nk)),
+        copy_out,
         out_shape=(jax.ShapeDtypeStruct(flow.shape, f32), jax.ShapeDtypeStruct(pres.shape, f32)),
-        in_specs=[vmem] * 3,
+        in_specs=[vmem] * 2,
         out_specs=(hbm, hbm),
-        scratch_shapes=[
-            pltpu.VMEM(flow.shape[1:], f32),
-            pltpu.VMEM(pres.shape[1:], f32),
-            pltpu.SemaphoreType.DMA((2, 2)),
-        ],
+        scratch_shapes=[pltpu.SemaphoreType.DMA((4,))],
         compiler_params=pltpu.CompilerParams(vmem_limit_bytes=32 * 1024 * 1024),
-    )(pad, coef, geo)
+    )(vel_new, pres_new)
 
 
 def solution(mesh):

time: 22.2 us -> 19.8 us (0.89)
  Pallas kernels: 21.3 us -> 18.9 us
    pallas_call x1, Pallas kernels: 19.8 us -> 18.2 us  [body(): pl.pallas_call(functools.partial(kernel, (tc, ac, nk, lon, colat, slots,...]
    pallas_call x1, Pallas kernels: 1.53 us -> 0.78 us  [body(): pl.pallas_call(copy_out, out_shape=(jax.ShapeDtypeStruct(flow.shape, f32)...]
where the time goes in v3:
time: 19.8 us; the launch traced here: 19.6 us
  Pallas kernels  18.9 us (95%)
  between operations  0.64 us (3%)
    pallas_call x1, Pallas kernels, body(): pl.pallas_call(functools.partial(kernel, (tc, ac, nk, lon, colat, slots,...  18.2 us
    pallas_call x1, Pallas kernels, body(): pl.pallas_call(copy_out, out_shape=(jax.ShapeDtypeStruct(flow.shape, f32)...  0.78 us

profile of v3, /device:TPU:0, one launch (start us, length us, event | category | flops | bytes accessed | tf_op | source)
XLA Modules:
  0.0 19.6 jit_solution(1811682828281108545)
XLA Ops:
  0.6 18.2 %shard_map.113 = (f32[3,8,24,128]{3,2,1,0:T(8,128)S(1)}, f32[8,24,128]{2,1,0:T(8,128)S(1)}) custom-call(f32[128]{0:T(128)} %constant.4.clone.polar_hbm, s32[3,416]{1,0:T(4,128)} %constant.5.clone.const_hbm, s32[1,416]{1,0:T(1,128)} %portion_hbm.1, s32[1,416]{1,0:T(1,128)} %slot_hbm.1, f32[1,2,416]{2,1,0:T(2,128)} %weight_hbm.1, f32[1,416]{1,0:T(1,128)} %angle_hbm.1, ...), custom_call_target="tpu_custom_call" | custom-call | tf_op jit(solution)/shard_map/pallas_call | solution.py:542
  18.8 0.8 %shard_map.114 = (f32[1,3,8,24,128]{4,3,2,1,0:T(8,128)}, f32[1,8,24,128]{3,2,1,0:T(8,128)}) custom-call(f32[3,8,24,128]{3,2,1,0:T(8,128)S(1)} %get-tuple-element.4.vel, f32[8,24,128]{2,1,0:T(8,128)S(1)} %get-tuple-element.5.pres), custom_call_target="tpu_custom_call" | custom-call | tf_op jit(solution)/shard_map/pallas_call | solution.py:580

commit v4 on v3

--- a/solution.py
+++ b/solution.py
@@ -306,15 +306,14 @@
 
     def gather(sweep):
         pad, send, n = pads[sweep], sends[sweep], counts[sweep]
-        fields = [
-            jnp.dot(
-                blend,
-                pad[f, 1 : tc + 1, inner, :].reshape(cells, nk),
-                precision=HIGHEST,
-                preferred_element_type=jnp.float32,
-            )
-            for f in range(n)
-        ]
+        donors = [pad[f, 1 : tc + 1, inner, :].reshape(cells, nk) for f in range(n)]
+        blended = jnp.dot(
+            blend,
+            jnp.concatenate(donors, axis=1),
+            precision=HIGHEST,
+            preferred_element_type=jnp.float32,
+        )
+        fields = [blended[:, f * nk : (f + 1) * nk] for f in range(n)]
         polar, azimuth = fields[1], fields[2]
         fields[1] = cosine * polar + sine * azimuth
         fields[2] = cosine * azimuth - sine * polar
@@ -390,21 +389,21 @@
     def assemble(sweep, where_to):
         pad, recv, n = pads[sweep], recvs[sweep], counts[sweep]
         sides, bands = [], []
-        for m in range(recv.shape[1]):
-            if m * pack >= n:
-                continue
-            rest = recv[:, m].reshape(packed, nk)
-            placed = None
-            for _ in range(3):
-                part = rest.astype(jnp.bfloat16)
-                rest = rest - part.astype(jnp.float32)
-                term = lax.dot_general(
-                    where_to,
-                    part,
-                    (((0,), (0,)), ((), ())),
-                    preferred_element_type=jnp.float32,
-                )
-                placed = term if placed is None else placed + term
+        tiles = -(-n // pack)
+        rest = jnp.concatenate([recv[:, m].reshape(packed, nk) for m in range(tiles)], axis=1)
+        every = None
+        for _ in range(3):
+            part = rest.astype(jnp.bfloat16)
+            rest = rest - part.astype(jnp.float32)
+            term = lax.dot_general(
+                where_to,
+                part,
+                (((0,), (0,)), ((), ())),
+                preferred_element_type=jnp.float32,
+            )
+            every = term if every is None else every + term
+        for m in range(tiles):
+            placed = every[:, m * nk : (m + 1) * nk]
             for h in range(pack):
                 if m * pack + h < n:
                     mine = placed[h * ghosts : (h + 1) * ghosts]

time: 19.8 us -> 19.6 us (0.990)
  no operation moved by 1% of the time
where the time goes in v4:
time: 19.6 us; the launch traced here: 19.4 us
  Pallas kernels  18.8 us (96%)
  between operations  0.64 us (3%)
    pallas_call x1, Pallas kernels, body(): pl.pallas_call(functools.partial(kernel, (tc, ac, nk, lon, colat, slots,...  18 us
    pallas_call x1, Pallas kernels, body(): pl.pallas_call(copy_out, out_shape=(jax.ShapeDtypeStruct(flow.shape, f32)...  0.78 us

profile of v4, /device:TPU:0, one launch (start us, length us, event | category | flops | bytes accessed | tf_op | source)
XLA Modules:
  0.0 19.4 jit_solution(15484793136168383179)
XLA Ops:
  0.6 18.0 %shard_map.113 = (f32[3,8,24,128]{3,2,1,0:T(8,128)S(1)}, f32[8,24,128]{2,1,0:T(8,128)S(1)}) custom-call(f32[128]{0:T(128)} %constant.4.clone.polar_hbm, s32[3,416]{1,0:T(4,128)} %constant.5.clone.const_hbm, s32[1,416]{1,0:T(1,128)} %portion_hbm.1, s32[1,416]{1,0:T(1,128)} %slot_hbm.1, f32[1,2,416]{2,1,0:T(2,128)} %weight_hbm.1, f32[1,416]{1,0:T(1,128)} %angle_hbm.1, ...), custom_call_target="tpu_custom_call" | custom-call | tf_op jit(solution)/shard_map/pallas_call | solution.py:541
  18.6 0.8 %shard_map.114 = (f32[1,3,8,24,128]{4,3,2,1,0:T(8,128)}, f32[1,8,24,128]{3,2,1,0:T(8,128)}) custom-call(f32[3,8,24,128]{3,2,1,0:T(8,128)S(1)} %get-tuple-element.4.vel, f32[8,24,128]{2,1,0:T(8,128)S(1)} %get-tuple-element.5.pres), custom_call_target="tpu_custom_call" | custom-call | tf_op jit(solution)/shard_map/pallas_call | solution.py:579
